TPU v7x, 128 devices: a whole 4x4x4 slice. The times are simulated.
128 devices in a mesh: dp: 8 (over y, z_lo), mp: 16 (over z_hi, x, core).
Axes of the slice: x: 4, y: 4, z: 4 (z_hi: 2, z_lo: 2; z = z_hi * 2 + z_lo), core: 2. Of those that a mesh axis runs over, the one named last changes fastest.
Arguments:
- attn_values: bfloat16 [2048, 4096], P('dp', 'mp'), may hold values from -6 to 6
- out_proj: bfloat16 [4096, 4608], P('mp'), may hold values from -0.1875 to 0.1875
- post_gain: float32 [4608], replicated, may hold values from 0.1 to 1.9
- residual: bfloat16 [2048, 4608], P(('dp', 'mp')), may hold values from -8.5 to 8.5
- sae_weight: bfloat16 [4608, 32768], P(None, 'mp'), may hold values from -0.09375 to 0.09375
- enc_bias: float32 [32768], P('mp'), may hold values from -3 to 3
- dec_bias: float32 [4608], replicated, may hold values from -3 to 3
Outputs:
- stream: bfloat16 [2048, 4608], P(('dp', 'mp'))
- weight_grad: float32 [4608, 32768], P('dp', 'mp')
- enc_bias_grad: float32 [32768], P('mp')
- dec_bias_grad: float32 [4608], replicated
All inputs are finite; a program needn't handle non-finite values.
Results may differ from a plain program's by a relative error of at most 0.0095.
Values may be sent and summed in bfloat16 or wider, within the bound.
A program may use at most 192 MiB of HBM per device.

v0:
```python
import math

import jax
import jax.numpy as jnp
from jax import lax
from jax.sharding import PartitionSpec as P

SPARSITY = 0.5
LAST_CONTRACT = (((1,), (1,)), ((), ()))
FIRST_CONTRACT = (((0,), (0,)), ((), ()))


def rms_scale(values, post_gain):
    mean_sq = jnp.mean(values * values, axis=-1, keepdims=True)
    return values * lax.rsqrt(mean_sq + 1e-06) * post_gain


def per_device(attn_values, out_proj, post_gain, residual, sae_weight, enc_bias, dec_bias):
    tok_rows = attn_values.shape[0]
    own_rows = residual.shape[0]
    loss_scale = 1.0 / math.sqrt(tok_rows * lax.axis_size("dp"))
    partial_value = jnp.dot(attn_values, out_proj, preferred_element_type=jnp.float32)
    full_resid = lax.all_gather(residual, "mp", axis=0, tiled=True)
    attn_out = lax.psum(partial_value, "mp")
    stream_full = (full_resid.astype(jnp.float32) + rms_scale(attn_out, post_gain)).astype(
        jnp.bfloat16
    )
    stream_own = lax.dynamic_slice_in_dim(stream_full, lax.axis_index("mp") * own_rows, own_rows, 0)
    centered = (stream_full.astype(jnp.float32) - dec_bias).astype(jnp.bfloat16)
    preact = jnp.dot(centered, sae_weight, preferred_element_type=jnp.float32) + enc_bias
    positive = jnp.maximum(preact, 0.0)
    latent = (positive * positive).astype(jnp.bfloat16)
    recon_term = lax.dot_general(
        latent, sae_weight, LAST_CONTRACT, preferred_element_type=jnp.float32
    )
    recon = lax.psum(recon_term, "mp") + dec_bias
    err_grad = ((recon - stream_full.astype(jnp.float32)) * loss_scale).astype(jnp.bfloat16)
    lat_grad = (
        jnp.dot(err_grad, sae_weight, preferred_element_type=jnp.float32) + SPARSITY * loss_scale
    )
    pre_grad = (lat_grad * (2.0 * positive)).astype(jnp.bfloat16)
    enc_bias_grad, err_sum = lax.psum(
        (
            jnp.sum(pre_grad.astype(jnp.float32), axis=0),
            jnp.sum(err_grad.astype(jnp.float32), axis=0),
        ),
        "dp",
    )
    projected = jnp.dot(
        sae_weight.astype(jnp.float32), enc_bias_grad, precision=lax.Precision.HIGHEST
    )
    dec_bias_grad = err_sum - lax.psum(projected, "mp")
    term = lax.dot_general(centered, pre_grad, FIRST_CONTRACT, preferred_element_type=jnp.float32)
    weight_grad = lax.psum_scatter(
        (
            term
            + lax.dot_general(err_grad, latent, FIRST_CONTRACT, preferred_element_type=jnp.float32)
        ).astype(jnp.bfloat16),
        "dp",
        scatter_dimension=0,
        tiled=True,
    ).astype(jnp.float32)
    return (stream_own, weight_grad, enc_bias_grad, dec_bias_grad)


def solution(mesh):
    return jax.shard_map(
        per_device,
        mesh=mesh,
        in_specs=(
            P("dp", "mp"),
            P("mp", None),
            P(),
            P(("dp", "mp"), None),
            P(None, "mp"),
            P("mp"),
            P(),
        ),
        out_specs=(P(("dp", "mp"), None), P("dp", "mp"), P("mp"), P()),
        check_vma=False,
    )
```

profile of v0, /device:TPU:0, one launch (start us, length us, event | category | flops | bytes accessed | tf_op | source)
XLA Modules:
  0.0 826.3 jit_solution(1997583626899708555)
XLA Ops:
  7.2 0.0 copy-start
  7.2 0.0 all-reduce.4.cloned.1.call-start
  7.2 1.6 copy-done
  8.8 3.9 fusion.11
  12.7 0.0 copy-start.6
  12.7 0.0 all-reduce.4.cloned.1.call-update
  12.7 0.0 all-gather.2.cloned.1.call-start
  12.8 0.7 all-gather.2.cloned.1.call-update
  13.5 0.0 all-reduce.6.cloned.1.call-start
  13.5 154.0 %all-reduce.4.cloned.1.call-done = f32[256,4608]{1,0:T(8,128)} async-done(((f32[256,4608]{1,0:T(8,128)}), f32[256,4608]{1,0:T(8,128)}) %all-reduce.4.cloned.1.call-update) | async-done | bytes 4718608 | tf_op jit(solution)/shard_map/psum | solution.py:24
  167.5 2.7 multiply_reduce_fusion
  170.3 0.0 copy-start.5
  170.3 0.0 copy-start.8
  170.3 49.7 %all-gather.2.cloned.1.call-done = bf16[256,4608]{1,0:T(8,128)(2,1)} async-done(((bf16[16,4608]{1,0:T(8,128)(2,1)}), bf16[256,4608]{1,0:T(8,128)(2,1)}) %all-gather.2.cloned.1.call-update) | async-done | bytes 2359312 | tf_op jit(solution)/shard_map/all_gather | solution.py:23
  220.0 0.0 copy-done.6
  220.0 3.9 add_convert_fusion.1
  223.9 0.0 copy-done.5
  224.0 0.0 copy-done.8
  224.0 9.0 %fusion.4 = f32[256,2048]{1,0:T(8,128)S(1)} fusion(bf16[4608,2048]{1,0:T(8,128)(2,1)} %param.11, bf16[256,4608]{1,0:T(8,128)(2,1)S(1)} %add_convert_fusion.1, f32[4608]{0:T(1024)S(1)} %copy-done.5, f32[2048]{0:T(1024)S(1)} %copy-done.8), kind=kOutput, calls=%fused_computation.12 | convolution fusion | flops 4836425728 | bytes 23357440 | tf_op jit(solution)/shard_map/dot_general | solution.py:30
  233.0 0.0 copy-start.3
  233.0 1.3 copy-done.3
  234.3 11.2 %fusion.9 = f32[256,4608]{1,0:T(8,128)} fusion(bf16[4608,2048]{1,0:T(8,128)(2,1)} %param.11, f32[256,2048]{1,0:T(8,128)S(1)} %fusion.4), kind=kOutput, calls=%fused_computation.18 | convolution fusion | flops 4832886784 | bytes 25690112 | tf_op jit(solution)/shard_map/dot_general | solution.py:33
  245.5 0.0 all-reduce.6.cloned.1.call-update
  245.5 0.2 reduce-scatter.2.cloned.1.call-start
  245.8 150.6 %all-reduce.6.cloned.1.call-done = f32[256,4608]{1,0:T(8,128)} async-done(((f32[256,4608]{1,0:T(8,128)}), f32[256,4608]{1,0:T(8,128)}) %all-reduce.6.cloned.1.call-update) | async-done | bytes 4718608 | tf_op jit(solution)/shard_map/psum | solution.py:36
  396.4 0.0 copy-start.4
  396.4 3.4 convert_reduce_fusion
  399.8 0.0 copy-start.2
  399.8 0.0 copy-done.4
  399.9 10.3 %convert_reduce_fusion.1 = (f32[2048]{0:T(1024)S(1)}, bf16[256,2048]{1,0:T(8,128)(2,1)S(1)}) fusion(f32[256,2048]{1,0:T(8,128)S(1)} %copy-done.4, bf16[256,4608]{1,0:T(8,128)(2,1)S(1)} %get-tuple-element.7, bf16[4608,2048]{1,0:T(8,128)(2,1)} %param.11), kind=kOutput, calls=%fused_computation.14 | convolution fusion | flops 4834981888 | bytes 24387584 | tf_op jit(solution)/shard_map/dot_general | solution.py:39
  410.2 0.0 copy-done.2
  410.2 14.8 %fusion.6 = f32[4608,2048]{1,0:T(8,128)} fusion(bf16[256,2048]{1,0:T(8,128)(2,1)S(1)} %get-tuple-element.9, bf16[256,4608]{1,0:T(8,128)(2,1)S(1)} %add_convert_fusion.1, f32[4608]{0:T(1024)S(1)} %copy-done.5), kind=kOutput, calls=%fused_computation.16 | convolution fusion | flops 4835377152 | bytes 41175040 | tf_op jit(solution)/shard_map/dot_general | solution.py:53
  425.0 22.1 %add_convert_fusion = bf16[4608,2048]{1,0:T(8,128)(2,1)} fusion(f32[4608,2048]{1,0:T(8,128)} %fusion.6, bf16[256,4608]{1,0:T(8,128)(2,1)} %copy-done.2, f32[256,2048]{1,0:T(8,128)} %copy-done.3), kind=kOutput, calls=%fused_computation | convolution fusion | flops 4851761152 | bytes 61079552 | tf_op jit(solution)/shard_map/dot_general | solution.py:57
  447.1 0.0 reduce-scatter.2.cloned.1.call-update
  447.1 0.7 constant_dynamic-slice_fusion
  447.8 50.1 %all-reduce = (f32[2048]{0:T(1024)S(1)}, f32[4608]{0:T(1024)S(1)}) all-reduce(f32[2048]{0:T(1024)S(1)} %get-tuple-element.8, f32[4608]{0:T(1024)S(1)} %get-tuple-element.6), channel_id=1, replica_groups=mesh['dp'=8,'mp'=16] {'dp'}, use_global_device_ids=true, to_apply=%region_5.0 | all-reduce | flops 6656 | bytes 53248 | tf_op jit(solution)/shard_map/psum | solution.py:42
  497.9 0.0 copy-start.7
  497.9 0.0 copy-start.1
  497.9 18.7 %convolution_reduce_fusion = f32[4608]{0:T(1024)S(1)} fusion(f32[2048,1]{0,1:T(1,128)S(1)} %bitcast.11, bf16[4608,2048]{1,0:T(8,128)(2,1)} %param.11), kind=kOutput, calls=%fused_computation.17 | convolution fusion | flops 113246208 | bytes 18900992 | tf_op jit(solution)/shard_map/dot_general | solution.py:49
  516.6 0.0 copy-done.7
  516.6 66.6 %psum.39 = f32[4608]{0:T(1024)S(1)} all-reduce(f32[4608]{0:T(1024)S(1)} %convolution_reduce_fusion), channel_id=1, replica_groups=mesh['dp'=8,'mp'=16] {'mp'}, use_global_device_ids=true, to_apply=%region_8.0 | all-reduce | flops 4608 | bytes 36864 | tf_op jit(solution)/shard_map/psum | solution.py:52
  583.2 0.6 sub.17
  583.8 231.4 %reduce-scatter.2.cloned.1.call-done = bf16[576,2048]{1,0:T(8,128)(2,1)} async-done(((bf16[4608,2048]{1,0:T(8,128)(2,1)}), bf16[576,2048]{1,0:T(8,128)(2,1)}) %reduce-scatter.2.cloned.1.call-update) | async-done | bytes 2359312 | tf_op jit(solution)/shard_map/reduce_scatter | solution.py:54
  815.3 4.5 convert_element_type.43
  819.7 0.0 copy-done.1
  (1 shorter events, 0.0 us)
Async XLA Ops:
  7.2 1.7 copy-start
  7.2 160.3 %all-reduce.4.cloned.1.call-start = ((), (), s32[]{:S(2)}) async-start(), calls=%async_computation.2 | async-start | bytes 9437184 | tf_op jit(solution)/shard_map/psum | solution.py:24
  12.7 207.3 %copy-start.6 = (f32[4608]{0:T(1024)S(1)}, f32[4608]{0:T(1024)}, u32[]{:S(2)}) copy-start(f32[4608]{0:T(1024)} %param.9) | copy-start | bytes 55300
  12.7 207.3 %all-gather.2.cloned.1.call-start = ((), (), s32[]{:S(2)}) async-start(), calls=%async_computation.1 | async-start | bytes 2506752 | tf_op jit(solution)/shard_map/all_gather | solution.py:23
  13.5 382.9 %all-reduce.6.cloned.1.call-start = ((), (), s32[]{:S(2)}) async-start(), calls=%async_computation.3 | async-start | bytes 9437184 | tf_op jit(solution)/shard_map/psum | solution.py:36
  170.3 53.7 %copy-start.5 = (f32[4608]{0:T(1024)S(1)}, f32[4608]{0:T(1024)}, u32[]{:S(2)}) copy-start(f32[4608]{0:T(1024)} %param.13) | copy-start | bytes 55300
  170.3 53.7 %copy-start.8 = (f32[2048]{0:T(1024)S(1)}, f32[2048]{0:T(1024)}, u32[]{:S(2)}) copy-start(f32[2048]{0:T(1024)} %param.12) | copy-start | bytes 24580
  233.0 1.3 copy-start.3
  245.5 569.8 %reduce-scatter.2.cloned.1.call-start = ((), (), s32[]{:S(2)}) async-start(), calls=%async_computation.4 | async-start | bytes 21233664 | tf_op jit(solution)/shard_map/reduce_scatter | solution.py:54
  396.4 3.4 copy-start.4
  399.8 10.4 %copy-start.2 = (bf16[256,4608]{1,0:T(8,128)(2,1)}, bf16[256,4608]{1,0:T(8,128)(2,1)S(1)}, u32[]{:S(2)}) copy-start(bf16[256,4608]{1,0:T(8,128)(2,1)S(1)} %get-tuple-element.7) | copy-start | bytes 7077892
  497.9 18.7 %copy-start.7 = (f32[2048]{0:T(1024)}, f32[2048]{0:T(1024)S(1)}, u32[]{:S(2)}) copy-start(f32[2048]{0:T(1024)S(1)} %get-tuple-element.4) | copy-start | bytes 24580
  497.9 321.9 %copy-start.1 = (bf16[256,4608]{1,0:T(8,128)(2,1)S(1)}, bf16[256,4608]{1,0:T(8,128)(2,1)}, u32[]{:S(2)}) copy-start(bf16[256,4608]{1,0:T(8,128)(2,1)} %param.8) | copy-start | bytes 7077892
Sparse Core Ops, SparseCore 0:
  12.9 154.6 all-reduce.3
  169.9 50.0 all-gather.1
  245.7 150.6 all-reduce.5
  447.2 368.0 reduce-scatter.1
where the time goes:
time: 827 us; the launch traced here: 826 us
  waiting for transfers between devices  586 us (71%)
  blocking collectives  117 us (14%)
  matrix products  90 us (11%)
  other arithmetic  15.2 us (2%)
  between operations  13.9 us (2%)
    reduce_scatter x1, waiting for transfers between devices, per_device(): lax.psum_scatter((term + lax.dot_general(err_grad, latent, FIRST_CONTRACT...  231 us
    psum x1, waiting for transfers between devices, per_device(): attn_out = lax.psum(partial_value, 'mp')  154 us
    psum x1, waiting for transfers between devices, per_device(): recon = lax.psum(recon_term, 'mp') + dec_bias  151 us
    psum x1, blocking collectives, per_device(): dec_bias_grad = err_sum - lax.psum(projected, 'mp')  66.6 us
    psum x1, blocking collectives, per_device(): lax.psum((jnp.sum(pre_grad.astype(jnp.float32), axis=0), jnp.sum(err_grad...  50.1 us
    all_gather x1, waiting for transfers between devices, per_device(): full_resid = lax.all_gather(residual, 'mp', axis=0, tiled=True)  49.7 us
    dot_general x1, matrix products, per_device(): lax.dot_general(err_grad, latent, FIRST_CONTRACT, preferred_element_type=...  22.1 us
    dot_general x1, matrix products, per_device(): jnp.dot(sae_weight.astype(jnp.float32), enc_bias_grad, precision=lax.Prec...  18.7 us
  transfers between devices with their start and end apart: 4, of which 4 were waited for; matrix products, arithmetic and copies ran while one was open for 3% of the time, Pallas kernels for 0%

commit v1 on v0

v1 whole, which is shorter than its diff:
```python
import math

import jax
import jax.numpy as jnp
from jax import lax
from jax.experimental import pallas as pl
from jax.experimental.pallas import tpu as pltpu
from jax.sharding import PartitionSpec as P

SPARSITY = 0.5
D = 4608
LAT = 1024
HALF = D // 2
ROWS = 16
TOK = 512
QROWS = D // 4
SUB = QROWS // 3
OWN = QROWS // 2
TOKENS = 2048
SCALE = 1.0 / math.sqrt(TOKENS)
F32 = jnp.float32
BF16 = jnp.bfloat16
H0 = pl.ds(0, HALF)
H1 = pl.ds(HALF, HALF)
LAST = (((1,), (1,)), ((), ()))
FIRST = (((0,), (0,)), ((), ()))


def kernel(
    attn, oproj, gain, resid, w_hbm, ebias, dbias,
    stream, wgrad, enc_out, dec_out,
    w_v, cen, err, pos, lat, pre,
    rsend, rown, rrecv, p1recv, p1r2,
    rz, rx, s2a, s2b, r2a, r2b,
    ysend, yrecv, zsend, zrecv, tmp,
    es3, esr, ezr, dcore, dx_r, dz_r, dy_r,
    w_sem, p1_s, p1_r, p2_s, p2_r, ag_s, ag_r, rc_s, rc_r, r1_s, r1_r, r2_s, r2_r,
    y_s, y_r, z_s, z_r, b_s, b_r,
):
    dp, mp = lax.axis_index("dp"), lax.axis_index("mp")
    y, zl = dp // 2, dp % 2
    zh, x, c = mp // 8, (mp // 2) % 4, mp % 2
    z = zh * 2 + zl

    def dev(x_, y_, z_, c_):
        return (y_ * 2 + z_ % 2, (z_ // 2) * 8 + x_ * 2 + c_)

    core = dev(x, y, z, 1 - c)

    def xpeer(k):
        return dev((x + k) % 4, y, z, c)

    def zpeer(k):
        return dev(x, y, (z + k) % 4, c)

    def ypeer(k):
        return dev(x, (y + k) % 4, z, c)

    zpart = dev(x, y, zh * 2 + 1 - zl, c)

    def far(j):
        return dev((x + j % 4) % 4, y, ((zh + j // 4) % 2) * 2 + zl, c)

    def remote(src, dst, ssem, rsem, to):
        return pltpu.make_async_remote_copy(
            src_ref=src, dst_ref=dst, send_sem=ssem, recv_sem=rsem,
            device_id=to, device_id_type=pl.DeviceIdType.MESH,
        )

    w_copy = pltpu.make_async_copy(
        w_hbm.at[:, pl.ds(pl.multiple_of(zl * LAT, LAT), LAT)], w_v, w_sem
    )
    w_copy.start()

    barrier = pltpu.get_barrier_semaphore()
    partners = [core]
    for k in (1, 2, 3):
        partners += [xpeer(k), zpeer(k), ypeer(k), far(4 + k)]
    for to in partners:
        pl.semaphore_signal(barrier, inc=1, device_id=to, device_id_type=pl.DeviceIdType.MESH)
    pl.semaphore_wait(barrier, len(partners))

    def proj(which):
        return attn[:, :, pl.ds(which, 1)].reshape(128, 256)

    def peer_proj(j, carry):
        cols = pl.ds(pl.multiple_of(j * 512, 512), 512)
        part = jnp.dot(proj(1 - c), oproj[:, cols], preferred_element_type=F32)
        rsend[pl.ds(0, 2), :, :, cols] = part.astype(BF16).reshape(2, 4, ROWS, 512)
        return carry

    lax.fori_loop(0, 9, peer_proj, 0)
    p1 = remote(rsend.at[pl.ds(0, 2)], p1recv, p1_s, p1_r, core)
    p1.start()

    def own_proj(j, carry):
        cols = pl.ds(pl.multiple_of(j * 512, 512), 512)
        part = jnp.dot(proj(c), oproj[:, cols], preferred_element_type=F32)
        rown[pl.ds(0, 2), :, :, cols] = part.reshape(2, 4, ROWS, 512)
        return carry

    lax.fori_loop(0, 9, own_proj, 0)
    p1.wait()

    def add_proj(j, carry):
        total = rown[j // 4, j % 4] + p1recv[j // 4, j % 4].astype(F32)
        rown[j // 4, j % 4] = total
        p1recv[j // 4, j % 4] = total.astype(BF16)
        return carry

    lax.fori_loop(0, 8, add_proj, 0)
    p2 = [
        remote(
            p1recv.at[(zh + j // 4) % 2, (x + j % 4) % 4], p1r2.at[j - 1],
            p2_s.at[j - 1], p2_r.at[j - 1], far(j),
        )
        for j in range(1, 8)
    ]
    for copy in p2:
        copy.start()
    for copy in p2:
        copy.wait()
    attn_out = rown[zh, x]
    for j in range(7):
        attn_out = attn_out + p1r2[j].astype(F32)
    mean_sq = jnp.mean(attn_out * attn_out, axis=-1, keepdims=True)
    normed = attn_out * lax.rsqrt(mean_sq + 1e-06) * gain[...]
    own_stream = (resid[...].astype(F32) + normed).astype(BF16)
    stream[...] = own_stream
    cen[c, z, x] = (own_stream.astype(F32) - dbias[...]).astype(BF16)

    def gather(buf, phase):
        s_sem, r_sem = ag_s.at[phase], ag_r.at[phase]
        own_z = buf.at[c, z, :, :, H0]
        own_x = buf.at[c, :, x, :, H1]
        first = []
        for k in (1, 2, 3):
            mine = buf.at[c, z, x, :, H0]
            first.append(remote(mine, mine, s_sem.at[k], r_sem.at[k], xpeer(k)))
            mine = buf.at[c, z, x, :, H1]
            first.append(remote(mine, mine, s_sem.at[3 + k], r_sem.at[3 + k], zpeer(k)))
        for copy in first:
            copy.start()
        for copy in first:
            copy.wait()
        second = []
        for k in (1, 2, 3):
            second.append(remote(own_z, own_z, s_sem.at[6 + k], r_sem.at[6 + k], zpeer(k)))
            second.append(remote(own_x, own_x, s_sem.at[9 + k], r_sem.at[9 + k], xpeer(k)))
        for copy in second:
            copy.start()
        third = [
            remote(own_z, own_z, s_sem.at[13], r_sem.at[13], core),
            remote(own_x, own_x, s_sem.at[14], r_sem.at[14], core),
        ]
        for copy in third:
            copy.start()
        for k in (1, 2, 3):
            second[2 * k - 2].wait()
            came = buf.at[c, (z + 4 - k) % 4, :, :, H0]
            third.append(remote(came, came, s_sem.at[14 + k], r_sem.at[14 + k], core))
            third[-1].start()
            second[2 * k - 1].wait()
            came = buf.at[c, :, (x + 4 - k) % 4, :, H1]
            third.append(remote(came, came, s_sem.at[17 + k], r_sem.at[17 + k], core))
            third[-1].start()
        for copy in third:
            copy.wait()

    gather(cen, 0)
    w_copy.wait()

    def encode(n, carry):
        cols = pl.ds(pl.multiple_of(n * 256, 256), 256)
        act = jnp.dot(cen[...].reshape(TOK, D), w_v[:, cols], preferred_element_type=F32)
        act = jnp.maximum(act + ebias[pl.ds(zl, 1), cols], 0.0)
        pos[:, cols] = act
        lat[:, cols] = (act * act).astype(BF16)
        return carry

    lax.fori_loop(0, 4, encode, 0)

    def decode(which, j):
        cols = pl.ds(pl.multiple_of(j * 256, 256), 256)
        rows = lat[pl.ds(pl.multiple_of(which * 256, 256), 256), :]
        part = lax.dot_general(rows, w_v[cols, :], LAST, preferred_element_type=F32)
        return cols, part.reshape(4, 4, ROWS, 256)

    def peer_decode(j, carry):
        cols, part = decode(1 - c, j)
        rsend[:, :, :, cols] = part.astype(BF16)
        return carry

    def own_decode(j, carry):
        cols, part = decode(c, j)
        rown[:, :, :, cols] = part
        return carry

    rc = []
    for h, cols in enumerate((H0, H1)):
        lax.fori_loop(9 * h, 9 * h + 9, peer_decode, 0)
        rc.append(
            remote(rsend.at[:, :, :, cols], rrecv.at[:, :, :, cols], rc_s.at[h], rc_r.at[h], core)
        )
        rc[-1].start()
    r1 = []
    for h, cols in enumerate((H0, H1)):
        lax.fori_loop(9 * h, 9 * h + 9, own_decode, 0)
        rc[h].wait()

        def add_decode(j, carry, cols=cols):
            total = rown[j // 4, j % 4, :, cols] + rrecv[j // 4, j % 4, :, cols].astype(F32)
            rown[j // 4, j % 4, :, cols] = total
            rrecv[j // 4, j % 4, :, cols] = total.astype(BF16)
            return carry

        lax.fori_loop(0, 16, add_decode, 0)
        for k in (1, 2, 3):
            if h == 0:
                src, dst, to = rrecv.at[(z + k) % 4, :, :, H0], rz.at[k - 1], zpeer(k)
            else:
                src, dst, to = rrecv.at[:, (x + k) % 4, :, H1], rx.at[k - 1], xpeer(k)
            i = 3 * h + k - 1
            r1.append(remote(src, dst, r1_s.at[i], r1_r.at[i], to))
            r1[-1].start()
    r2 = []
    for h in (0, 1):
        for k in (1, 2, 3):
            r1[3 * h + k - 1].wait()
        for i in range(4):
            if h == 0:
                total = rown[z, i, :, H0]
                for k in range(3):
                    total = total + rz[k, i].astype(F32)
                rown[z, i, :, H0] = total
                s2a[i] = total.astype(BF16)
            else:
                total = rown[i, x, :, H1]
                for k in range(3):
                    total = total + rx[k, i].astype(F32)
                rown[i, x, :, H1] = total
                s2b[i] = total.astype(BF16)
        for k in (1, 2, 3):
            if h == 0:
                src, dst, to = s2a.at[(x + k) % 4], r2a.at[k - 1], xpeer(k)
            else:
                src, dst, to = s2b.at[(z + k) % 4], r2b.at[k - 1], zpeer(k)
            i = 3 * h + k - 1
            r2.append(remote(src, dst, r2_s.at[i], r2_r.at[i], to))
            r2[-1].start()
    err_sums = []
    for h, cols in enumerate((H0, H1)):
        for k in (1, 2, 3):
            r2[3 * h + k - 1].wait()
        total = rown[z, x, :, cols]
        for k in range(3):
            total = total + (r2a, r2b)[h][k].astype(F32)
        grad = (total + dbias[:, cols] - stream[:, cols].astype(F32)) * SCALE
        grad = grad.astype(BF16)
        err[c, z, x, :, cols] = grad
        dcore[pl.ds(c, 1), cols] = jnp.sum(grad.astype(F32), axis=0, keepdims=True)

    gather(err, 1)

    def back(n, carry):
        cols = pl.ds(pl.multiple_of(n * 256, 256), 256)
        grad = jnp.dot(err[...].reshape(TOK, D), w_v[:, cols], preferred_element_type=F32)
        grad = ((grad + SPARSITY * SCALE) * (2.0 * pos[:, cols])).astype(BF16)
        pre[:, cols] = grad
        esr[pl.ds(y, 1), cols] = jnp.sum(grad.astype(F32), axis=0, keepdims=True)
        return carry

    lax.fori_loop(0, 4, back, 0)

    def partial(q, sub, way):
        at = pl.ds(pl.multiple_of(q * QROWS + sub * SUB, SUB), SUB)
        cols = pl.ds(pl.multiple_of(way * 512, 512), 512)
        part = lax.dot_general(
            cen[:, :, :, :, at].reshape(TOK, SUB), pre[:, cols], FIRST, preferred_element_type=F32
        )
        return part + lax.dot_general(
            err[:, :, :, :, at].reshape(TOK, SUB), lat[:, cols], FIRST, preferred_element_type=F32
        )

    def sub_of(k):
        return 1 + (k - 1) * (2 * zl - 1)

    def ring(step, i):
        way = i % 2
        src = ysend.at[i] if step == 0 else yrecv.at[step - 1, i]
        to = dev(x, (y + 1 + 2 * way) % 4, z, c)
        return remote(src, yrecv.at[step, i], y_s.at[step, i], y_r.at[step, i], to)

    def owner(step, way):
        return (y + 7 - step + way * (2 * step + 2)) % 4

    def ring_step(step):
        def body(i, carry):
            k, way = i // 2, i % 2
            part = partial(owner(step, way), sub_of(k), way)
            if step == 0:
                ysend[i] = part.astype(BF16)
            else:
                ring(step - 1, i).wait_recv()
                yrecv[step - 1, i] = (yrecv[step - 1, i].astype(F32) + part).astype(BF16)
            ring(step, i).start()
            return carry

        lax.fori_loop(0, 6, body, 0)

    def b_copy(src, dst, i, to):
        return remote(src, dst, b_s.at[i], b_r.at[i], to)

    ring_step(0)

    own_sum = esr[pl.ds(y, 1), :]
    high = own_sum.astype(BF16)
    rest = own_sum - high.astype(F32)
    mid = rest.astype(BF16)
    low = (rest - mid.astype(F32)).astype(BF16)
    es3[...] = jnp.concatenate([high, mid, low, jnp.zeros((13, LAT), BF16)], axis=0)

    def project(j, carry):
        cols = pl.ds(pl.multiple_of(j * 512, 512), 512)
        part = lax.dot_general(es3[...], w_v[cols, :], LAST, preferred_element_type=F32)
        dcore[pl.ds(c, 1), cols] = dcore[pl.ds(c, 1), cols] - jnp.sum(part, axis=0, keepdims=True)
        return carry

    lax.fori_loop(0, 9, project, 0)
    bias = []
    mine = esr.at[pl.ds(y, 1)]
    for k in (1, 2, 3):
        bias.append(b_copy(mine, mine, k - 1, ypeer(k)))
    mine = dcore.at[pl.ds(c, 1)]
    bias.append(b_copy(mine, mine, 3, core))
    for copy in bias:
        copy.start()

    def dec_stage(slots, value, me, first, peer):
        slots[pl.ds(me, 1), :] = value
        mine = slots.at[pl.ds(me, 1)]
        out = [b_copy(mine, mine, first + k, peer(k + 1)) for k in range(3)]
        for copy in out:
            copy.start()
        return out

    def ordered(slots, count):
        total = slots[0:1, :]
        for i in range(1, count):
            total = total + slots[i : i + 1, :]
        return total

    ring_step(1)
    for copy in bias:
        copy.wait()
    ezr[pl.ds(zl, 1), :] = ordered(esr, 4)
    mine = ezr.at[pl.ds(zl, 1)]
    enc = b_copy(mine, mine, 4, zpart)
    enc.start()
    bias = dec_stage(dx_r, ordered(dcore, 2), x, 5, xpeer)
    ring_step(2)
    for copy in bias:
        copy.wait()
    bias = dec_stage(dz_r, ordered(dx_r, 4), z, 8, zpeer)
    enc.wait()
    enc_out[...] = ezr[...]

    other = 1 - zl
    own_cols = zl * LAT

    def zcopy(k, way):
        cols = pl.ds(pl.multiple_of(way * 512, 512), 512)
        if k == 0:
            rows = pl.ds(pl.multiple_of(192 * other, 64), SUB)
        else:
            rows = pl.ds(pl.multiple_of(SUB * zl, 64), 192)
        return remote(
            zsend.at[rows, cols], zrecv.at[rows, cols],
            z_s.at[2 * k + way], z_r.at[2 * k + way], zpart,
        )

    for k in range(3):

        def finish(way, carry, k=k):
            i = 2 * k + way
            cols = pl.ds(pl.multiple_of(way * 512, 512), 512)
            out_cols = pl.ds(pl.multiple_of(own_cols + way * 512, 512), 512)
            part = partial(y, sub_of(k), way)
            ring(2, i).wait_recv()
            total = yrecv[2, i].astype(F32) + part
            if k == 0:
                rows = pl.ds(pl.multiple_of(192 * other, 64), SUB)
                zsend[rows, cols] = total.astype(BF16)
                zcopy(0, way).start()
            elif k == 1:
                tmp[...] = total
                theirs = tmp[pl.ds(pl.multiple_of(192 * other, 64), 192), :]
                zsend[pl.ds(pl.multiple_of(SUB * zl, 64), 192), cols] = theirs.astype(BF16)
                zcopy(1, way).start()
                ours = tmp[pl.ds(pl.multiple_of(192 * zl, 64), 192), :]
                wgrad[pl.ds(pl.multiple_of(SUB * other, 64), 192), out_cols] = ours
            else:
                wgrad[pl.ds(pl.multiple_of(192 * zl, 64), SUB), out_cols] = total
            return carry

        lax.fori_loop(0, 2, finish, 0)
        if k == 0:
            for copy in bias:
                copy.wait()
            bias = dec_stage(dy_r, ordered(dz_r, 4), y, 11, ypeer)
    for copy in bias:
        copy.wait()
    dec_out[...] = ordered(dy_r, 4)

    def drain(i, carry):
        for step in range(3):
            ring(step, i).wait_send()
        return carry

    lax.fori_loop(0, 6, drain, 0)
    for k in (0, 1):
        for way in (0, 1):
            zcopy(k, way).wait()

    def widen(j, carry):
        rows = pl.ds(pl.multiple_of(j * 96, 32), 96)
        wgrad[rows, pl.ds(pl.multiple_of(other * LAT, LAT), LAT)] = zrecv[rows, :].astype(F32)
        return carry

    lax.fori_loop(0, 6, widen, 0)


def per_device(attn_values, out_proj, post_gain, residual, sae_weight, enc_bias, dec_bias):
    vmem = pl.BlockSpec(memory_space=pltpu.VMEM)
    hbm = pl.BlockSpec(memory_space=pl.ANY)
    block = (4, 4, ROWS, D)
    dma = pltpu.SemaphoreType.DMA
    stream, wgrad, enc, dec = pl.pallas_call(
        kernel,
        out_shape=(
            jax.ShapeDtypeStruct((ROWS, D), BF16),
            jax.ShapeDtypeStruct((OWN, 2 * LAT), F32),
            jax.ShapeDtypeStruct((2, LAT), F32),
            jax.ShapeDtypeStruct((1, D), F32),
        ),
        in_specs=[vmem, vmem, vmem, vmem, hbm, vmem, vmem],
        out_specs=(vmem, vmem, vmem, vmem),
        scratch_shapes=[
            pltpu.VMEM((D, LAT), BF16),
            pltpu.VMEM((2,) + block, BF16),
            pltpu.VMEM((2,) + block, BF16),
            pltpu.VMEM((TOK, LAT), F32),
            pltpu.VMEM((TOK, LAT), BF16),
            pltpu.VMEM((TOK, LAT), BF16),
            pltpu.VMEM(block, BF16),
            pltpu.VMEM(block, F32),
            pltpu.VMEM(block, BF16),
            pltpu.VMEM((2, 4, ROWS, D), BF16),
            pltpu.VMEM((7, ROWS, D), BF16),
            pltpu.VMEM((3, 4, ROWS, HALF), BF16),
            pltpu.VMEM((3, 4, ROWS, HALF), BF16),
            pltpu.VMEM((4, ROWS, HALF), BF16),
            pltpu.VMEM((4, ROWS, HALF), BF16),
            pltpu.VMEM((3, ROWS, HALF), BF16),
            pltpu.VMEM((3, ROWS, HALF), BF16),
            pltpu.VMEM((6, SUB, 512), BF16),
            pltpu.VMEM((3, 6, SUB, 512), BF16),
            pltpu.VMEM((OWN, LAT), BF16),
            pltpu.VMEM((OWN, LAT), BF16),
            pltpu.VMEM((SUB, 512), F32),
            pltpu.VMEM((16, LAT), BF16),
            pltpu.VMEM((4, LAT), F32),
            pltpu.VMEM((2, LAT), F32),
            pltpu.VMEM((2, D), F32),
            pltpu.VMEM((4, D), F32),
            pltpu.VMEM((4, D), F32),
            pltpu.VMEM((4, D), F32),
            dma, dma, dma, dma((7,)), dma((7,)), dma((2, 21)), dma((2, 21)),
            dma((2,)), dma((2,)), dma((6,)), dma((6,)), dma((6,)), dma((6,)),
            dma((3, 6)), dma((3, 6)), dma((4,)), dma((4,)), dma((14,)), dma((14,)),
        ],
        compiler_params=pltpu.CompilerParams(
            collective_id=0, has_side_effects=True, vmem_limit_bytes=63 * 2**20
        ),
        cost_estimate=pl.CostEstimate(
            flops=25 * 10**9, bytes_accessed=20 * 10**6, transcendentals=0
        ),
    )(
        attn_values.reshape(2, 4, 2, ROWS, 256),
        out_proj,
        post_gain.reshape(1, D),
        residual,
        sae_weight,
        enc_bias.reshape(2, LAT),
        dec_bias.reshape(1, D),
    )
    return stream, wgrad, enc.reshape(2 * LAT), dec.reshape(D)


def solution(mesh):
    return jax.shard_map(
        per_device,
        mesh=mesh,
        in_specs=(
            P("dp", "mp"),
            P("mp", None),
            P(),
            P(("dp", "mp"), None),
            P(None, "mp"),
            P("mp"),
            P(),
        ),
        out_specs=(P(("dp", "mp"), None), P("dp", "mp"), P("mp"), P()),
        check_vma=False,
    )
```

time: 827 us -> 233 us (0.28)
  waiting for transfers between devices: 586 us -> 0 us
  Pallas kernels: 0 us -> 218 us
  blocking collectives: 117 us -> 0 us
  matrix products: 90 us -> 0 us
  other arithmetic: 15.2 us -> 1.38 us
  between operations: 13.9 us -> 0.64 us
  local copies, waits for them, and re-layouts: 3.63 us -> 12 us
    psum x2 -> x0, waiting for transfers between devices: 305 us -> none  [the longest x1 154 us: per_device(): attn_out = lax.psum(partial_value, 'mp')]
    reduce_scatter x1 -> x0, waiting for transfers between devices: 231 us -> none  [per_device(): lax.psum_scatter((term + lax.dot_general(err_grad, latent, FIRST_CONTRACT...]
    pallas_call x0 -> x1, Pallas kernels: none -> 218 us  [per_device(): pl.pallas_call(kernel, out_shape=(jax.ShapeDtypeStruct((ROWS, D), BF16),...]
    psum x2 -> x0, blocking collectives: 117 us -> none  [the longest x1 66.6 us: per_device(): dec_bias_grad = err_sum - lax.psum(projected, 'mp')]
    dot_general x7 -> x0, matrix products: 90 us -> none  [the longest x1 22.1 us: per_device(): lax.dot_general(err_grad, latent, FIRST_CONTRACT, preferred_element_type=...]
    all_gather x1 -> x0, waiting for transfers between devices: 49.7 us -> none  [per_device(): full_resid = lax.all_gather(residual, 'mp', axis=0, tiled=True)]
    convert_element_type x2 -> x0, other arithmetic: 8.41 us -> none  [the longest x1 4.46 us: per_device(): weight_grad = lax.psum_scatter((term + lax.dot_general(err_grad, latent,...]
  transfers between devices with their start and end apart: 4 -> 0, of which waited for: 4 -> 0; matrix products, arithmetic and copies ran while one was open for 3% -> 0% of each run, Pallas kernels for 0% -> 0%
where the time goes in v1:
time: 233 us; the launch traced here: 232 us
  Pallas kernels  218 us (94%)
  local copies, waits for them, and re-layouts  12 us (5%)
    pallas_call x1, Pallas kernels, per_device(): pl.pallas_call(kernel, out_shape=(jax.ShapeDtypeStruct((ROWS, D), BF16),...  218 us
    unnamed x3, local copies, waits for them, and re-layouts  7.97 us

profile of v1, /device:TPU:0, one launch (start us, length us, event | category | flops | bytes accessed | tf_op | source)
XLA Modules:
  0.0 232.1 jit_solution(13764185475467312049)
XLA Ops:
  0.6 1.3 reshape.27.gain
  2.0 1.3 reshape.29.dbias
  3.3 1.3 reshape.28.ebias
  4.6 218.1 %shard_map.102 = (bf16[16,4608]{1,0:T(8,128)(2,1)}, f32[576,2048]{1,0:T(8,128)}, f32[2,1024]{1,0:T(2,128)}, f32[1,4608]{1,0:T(1,128)}) custom-call(bf16[2,4,2,16,256]{4,3,2,1,0:T(8,128)(2,1)} %bitcast.7, bf16[256,4608]{1,0:T(8,128)(2,1)} %oproj.1, f32[1,4608]{1,0:T(1,128)} %reshape.27.gain, bf16[16,4608]{1,0:T(8,128)(2,1)} %resid.1, ...), custom_call_target="tpu_custom_call" | custom-call | flops 24999999488 | bytes 20000000 | tf_op jit(solution)/shard_map/pallas_call | solution.py:438
  222.7 1.4 reduce
  224.1 1.3 copy.13
  225.4 1.6 copy.16
  227.0 5.1 %copy.17 = f32[576,2048]{1,0:T(8,128)} copy(f32[576,2048]{1,0:T(8,128)} %get-tuple-element.17) | data formatting | bytes 9437184

commit v2 on v1

v2 whole, which is shorter than its diff:
```python
import math

import jax
import jax.numpy as jnp
from jax import lax
from jax.experimental import pallas as pl
from jax.experimental.pallas import tpu as pltpu
from jax.sharding import PartitionSpec as P

SPARSITY = 0.5
D = 4608
LAT = 1024
HALF = D // 2
ROWS = 16
TOK = 512
QROWS = D // 4
SUB = QROWS // 3
OWN = QROWS // 2
TOKENS = 2048
SCALE = 1.0 / math.sqrt(TOKENS)
F32 = jnp.float32
BF16 = jnp.bfloat16
H0 = pl.ds(0, HALF)
H1 = pl.ds(HALF, HALF)
LAST = (((1,), (1,)), ((), ()))
FIRST = (((0,), (0,)), ((), ()))


def kernel(
    attn, oproj, gain, resid, w_hbm, ebias, dbias,
    stream, own_grad, zrecv, enc_out, dec_out,
    w_v, cen, err, cen_y, err_y, pos, lat, pre, lat_y, pre_y,
    rsend, rown, rrecv, p1r2,
    rz, rx, s2a, s2b, r2a, r2b,
    zsend, tmp,
    es3, esr, ezr, dcore, dx_r, dz_r, dy_r,
    w_sem, p1_s, p1_r, p2_s, p2_r, ag_s, ag_r, rc_s, rc_r, r1_s, r1_r, r2_s, r2_r,
    yp_s, yp_r, yl_s, yl_r, y_s, y_r, z_s, z_r, b_s, b_r,
):
    dp, mp = lax.axis_index("dp"), lax.axis_index("mp")
    y, zl = dp // 2, dp % 2
    zh, x, c = mp // 8, (mp // 2) % 4, mp % 2
    z = zh * 2 + zl

    def dev(x_, y_, z_, c_):
        return (y_ * 2 + z_ % 2, (z_ // 2) * 8 + x_ * 2 + c_)

    core = dev(x, y, z, 1 - c)

    def xpeer(k):
        return dev((x + k) % 4, y, z, c)

    def zpeer(k):
        return dev(x, y, (z + k) % 4, c)

    def ypeer(k):
        return dev(x, (y + k) % 4, z, c)

    zpart = dev(x, y, zh * 2 + 1 - zl, c)

    def far(j):
        return dev((x + j % 4) % 4, y, ((zh + j // 4) % 2) * 2 + zl, c)

    def remote(src, dst, ssem, rsem, to):
        return pltpu.make_async_remote_copy(
            src_ref=src, dst_ref=dst, send_sem=ssem, recv_sem=rsem,
            device_id=to, device_id_type=pl.DeviceIdType.MESH,
        )

    w_copy = pltpu.make_async_copy(
        w_hbm.at[:, pl.ds(pl.multiple_of(zl * LAT, LAT), LAT)], w_v, w_sem
    )
    w_copy.start()

    barrier = pltpu.get_barrier_semaphore()
    partners = [core]
    for k in (1, 2, 3):
        partners += [xpeer(k), zpeer(k), ypeer(k), far(4 + k)]
    for to in partners:
        pl.semaphore_signal(barrier, inc=1, device_id=to, device_id_type=pl.DeviceIdType.MESH)
    pl.semaphore_wait(barrier, len(partners))

    def proj(which):
        return attn[:, :, pl.ds(which, 1)].reshape(128, 256)

    def peer_proj(j, carry):
        cols = pl.ds(pl.multiple_of(j * 512, 512), 512)
        part = jnp.dot(proj(1 - c), oproj[:, cols], preferred_element_type=F32)
        rsend[pl.ds(0, 2), :, :, cols] = part.astype(BF16).reshape(2, 4, ROWS, 512)
        return carry

    lax.fori_loop(0, 9, peer_proj, 0)
    p1 = remote(rsend.at[pl.ds(0, 2)], rrecv.at[pl.ds(0, 2)], p1_s, p1_r, core)
    p1.start()

    def own_proj(j, carry):
        cols = pl.ds(pl.multiple_of(j * 512, 512), 512)
        part = jnp.dot(proj(c), oproj[:, cols], preferred_element_type=F32)
        rown[pl.ds(0, 2), :, :, cols] = part.reshape(2, 4, ROWS, 512)
        return carry

    lax.fori_loop(0, 9, own_proj, 0)
    p1.wait()

    def add_proj(j, carry):
        total = rown[j // 4, j % 4] + rrecv[j // 4, j % 4].astype(F32)
        rown[j // 4, j % 4] = total
        rrecv[j // 4, j % 4] = total.astype(BF16)
        return carry

    lax.fori_loop(0, 8, add_proj, 0)
    p2 = [
        remote(
            rrecv.at[(zh + j // 4) % 2, (x + j % 4) % 4], p1r2.at[j - 1],
            p2_s.at[j - 1], p2_r.at[j - 1], far(j),
        )
        for j in range(1, 8)
    ]
    for copy in p2:
        copy.start()
    for copy in p2:
        copy.wait()
    attn_out = rown[zh, x]
    for j in range(7):
        attn_out = attn_out + p1r2[j].astype(F32)
    mean_sq = jnp.mean(attn_out * attn_out, axis=-1, keepdims=True)
    normed = attn_out * lax.rsqrt(mean_sq + 1e-06) * gain[...].reshape(1, D)
    shift = dbias[...].reshape(1, D)
    own_stream = (resid[...].astype(F32) + normed).astype(BF16)
    stream[...] = own_stream
    cen[c, z, x] = (own_stream.astype(F32) - shift).astype(BF16)

    def gather(at, cut, width, phase):
        left, right = pl.ds(0, cut), pl.ds(cut, width - cut)
        every = slice(None)

        def copy(ref, i, to):
            return remote(ref, ref, ag_s.at[phase, i], ag_r.at[phase, i], to)

        first, second, third = [], [], []

        def begin():
            for k in (1, 2, 3):
                first.append(copy(at(z, x, left), k, xpeer(k)))
                first.append(copy(at(z, x, right), 3 + k, zpeer(k)))
            for one in first:
                one.start()

        def spread():
            for one in first:
                one.wait()
            for k in (1, 2, 3):
                second.append(copy(at(z, every, left), 6 + k, zpeer(k)))
                second.append(copy(at(every, x, right), 9 + k, xpeer(k)))
            third.append(copy(at(z, every, left), 13, core))
            third.append(copy(at(every, x, right), 14, core))
            for one in second + third:
                one.start()

        def share():
            for k in (1, 2, 3):
                second[2 * k - 2].wait()
                third.append(copy(at((z + 4 - k) % 4, every, left), 14 + k, core))
                third[-1].start()
                second[2 * k - 1].wait()
                third.append(copy(at(every, (x + 4 - k) % 4, right), 17 + k, core))
                third[-1].start()

        def end():
            for one in third:
                one.wait()

        return begin, spread, share, end

    def columns_of(buf, buf_y, phase):
        out = []
        for k in (1, 2, 3):
            theirs = pl.ds(pl.multiple_of(((y + k) % 4) * QROWS, 128), QROWS)
            out.append(
                remote(
                    buf.at[c, z, x, :, theirs], buf_y.at[k - 1, c, z, x],
                    yp_s.at[phase, k - 1], yp_r.at[phase, k - 1], ypeer(k),
                )
            )
        for copy in out:
            copy.start()
        return out

    def gather_both(buf, buf_y, phase):
        whole = gather(lambda z_, x_, cols: buf.at[c, z_, x_, :, cols], HALF, D, phase)
        part = gather(
            lambda z_, x_, cols: buf_y.at[:, c, z_, x_, :, cols], 640, QROWS, 2 + phase
        )
        whole[0]()
        out = columns_of(buf, buf_y, phase)
        whole[1]()
        for copy in out:
            copy.wait()
        part[0]()
        whole[2]()
        whole[3]()
        part[1]()
        return part

    cen_part = gather_both(cen, cen_y, 0)
    w_copy.wait()

    bias_row = ebias[...].reshape(2, LAT)
    bias_row = jnp.where(zl == 0, bias_row[0:1], bias_row[1:2])
    ezr[0:1, :] = bias_row

    def encode(n, carry):
        cols = pl.ds(pl.multiple_of(n * 256, 256), 256)
        act = jnp.dot(cen[...].reshape(TOK, D), w_v[:, cols], preferred_element_type=F32)
        act = jnp.maximum(act + ezr[0:1, cols], 0.0)
        pos[:, cols] = act
        lat[:, cols] = (act * act).astype(BF16)
        return carry

    lax.fori_loop(0, 4, encode, 0)
    lat_out = [
        remote(lat, lat_y.at[k - 1], yl_s.at[k - 1], yl_r.at[k - 1], ypeer(k)) for k in (1, 2, 3)
    ]
    for copy in lat_out:
        copy.start()

    def decode(which, j):
        cols = pl.ds(pl.multiple_of(j * 256, 256), 256)
        rows = lat[pl.ds(pl.multiple_of(which * 256, 256), 256), :]
        part = lax.dot_general(rows, w_v[cols, :], LAST, preferred_element_type=F32)
        return cols, part.reshape(4, 4, ROWS, 256)

    def peer_decode(j, carry):
        cols, part = decode(1 - c, j)
        rsend[:, :, :, cols] = part.astype(BF16)
        return carry

    def own_decode(j, carry):
        cols, part = decode(c, j)
        rown[:, :, :, cols] = part
        return carry

    rc = []
    for h, cols in enumerate((H0, H1)):
        lax.fori_loop(9 * h, 9 * h + 9, peer_decode, 0)
        rc.append(
            remote(rsend.at[:, :, :, cols], rrecv.at[:, :, :, cols], rc_s.at[h], rc_r.at[h], core)
        )
        rc[-1].start()
    cen_part[2]()
    r1 = []
    for h, cols in enumerate((H0, H1)):
        lax.fori_loop(9 * h, 9 * h + 9, own_decode, 0)
        rc[h].wait()

        def add_decode(j, carry, cols=cols):
            total = rown[j // 4, j % 4, :, cols] + rrecv[j // 4, j % 4, :, cols].astype(F32)
            rown[j // 4, j % 4, :, cols] = total
            rrecv[j // 4, j % 4, :, cols] = total.astype(BF16)
            return carry

        lax.fori_loop(0, 16, add_decode, 0)
        for k in (1, 2, 3):
            if h == 0:
                src, dst, to = rrecv.at[(z + k) % 4, :, :, H0], rz.at[k - 1], zpeer(k)
            else:
                src, dst, to = rrecv.at[:, (x + k) % 4, :, H1], rx.at[k - 1], xpeer(k)
            i = 3 * h + k - 1
            r1.append(remote(src, dst, r1_s.at[i], r1_r.at[i], to))
            r1[-1].start()
    r2 = []
    for h in (0, 1):
        for k in (1, 2, 3):
            r1[3 * h + k - 1].wait()
        for i in range(4):
            if h == 0:
                total = rown[z, i, :, H0]
                for k in range(3):
                    total = total + rz[k, i].astype(F32)
                rown[z, i, :, H0] = total
                s2a[i] = total.astype(BF16)
            else:
                total = rown[i, x, :, H1]
                for k in range(3):
                    total = total + rx[k, i].astype(F32)
                rown[i, x, :, H1] = total
                s2b[i] = total.astype(BF16)
        for k in (1, 2, 3):
            if h == 0:
                src, dst, to = s2a.at[(x + k) % 4], r2a.at[k - 1], xpeer(k)
            else:
                src, dst, to = s2b.at[(z + k) % 4], r2b.at[k - 1], zpeer(k)
            i = 3 * h + k - 1
            r2.append(remote(src, dst, r2_s.at[i], r2_r.at[i], to))
            r2[-1].start()
    for h, cols in enumerate((H0, H1)):
        for k in (1, 2, 3):
            r2[3 * h + k - 1].wait()
        total = rown[z, x, :, cols]
        for k in range(3):
            total = total + (r2a, r2b)[h][k].astype(F32)
        grad = (total + shift[:, h * HALF : (h + 1) * HALF] - stream[:, cols].astype(F32)) * SCALE
        grad = grad.astype(BF16)
        err[c, z, x, :, cols] = grad
        dcore[pl.ds(c, 1), cols] = jnp.sum(grad.astype(F32), axis=0, keepdims=True)

    err_part = gather_both(err, err_y, 1)

    def back(n, carry):
        cols = pl.ds(pl.multiple_of(n * 256, 256), 256)
        grad = jnp.dot(err[...].reshape(TOK, D), w_v[:, cols], preferred_element_type=F32)
        grad = ((grad + SPARSITY * SCALE) * (2.0 * pos[:, cols])).astype(BF16)
        pre[:, cols] = grad
        esr[pl.ds(y, 1), cols] = jnp.sum(grad.astype(F32), axis=0, keepdims=True)
        return carry

    near, onward = [], []

    def ycopy(src, dst, n, i, to):
        return remote(src, dst, y_s.at[n, i], y_r.at[n, i], to)

    def send_near(n):
        cols = pl.ds(n * 256, 256)
        near.append(
            [
                ycopy(pre.at[:, cols], pre_y.at[0, :, cols], n, 0, ypeer(1)),
                ycopy(pre.at[:, cols], pre_y.at[2, :, cols], n, 1, ypeer(3)),
            ]
        )
        for copy in near[n]:
            copy.start()

    def send_onward(n):
        cols, top, low = pl.ds(n * 256, 256), pl.ds(0, 256), pl.ds(256, 256)
        onward.append(
            [
                ycopy(pre_y.at[0, top, cols], pre_y.at[1, top, cols], n, 2, ypeer(1)),
                ycopy(pre_y.at[2, low, cols], pre_y.at[1, low, cols], n, 3, ypeer(3)),
            ]
        )
        for copy, came in zip(onward[n], near[n]):
            came.wait()
            copy.start()

    lax.fori_loop(0, 1, back, 0)
    send_near(0)
    lax.fori_loop(1, 2, back, 0)
    send_near(1)
    lax.fori_loop(2, 4, back, 0)

    own_sum = esr[pl.ds(y, 1), :]
    high = own_sum.astype(BF16)
    rest = own_sum - high.astype(F32)
    mid = rest.astype(BF16)
    bottom = (rest - mid.astype(F32)).astype(BF16)
    es3[...] = jnp.concatenate([high, mid, bottom, jnp.zeros((13, LAT), BF16)], axis=0)

    def b_copy(src, dst, i, to):
        return remote(src, dst, b_s.at[i], b_r.at[i], to)

    bias = []
    mine = esr.at[pl.ds(y, 1)]
    for k in (1, 2, 3):
        bias.append(b_copy(mine, mine, k - 1, ypeer(k)))
    for copy in bias:
        copy.start()

    def project(j, carry):
        cols = pl.ds(pl.multiple_of(j * 512, 512), 512)
        part = lax.dot_general(es3[...], w_v[cols, :], LAST, preferred_element_type=F32)
        dcore[pl.ds(c, 1), cols] = dcore[pl.ds(c, 1), cols] - jnp.sum(part, axis=0, keepdims=True)
        return carry

    lax.fori_loop(0, 9, project, 0)
    mine = dcore.at[pl.ds(c, 1)]
    bias.append(b_copy(mine, mine, 3, core))
    bias[-1].start()

    def dec_stage(slots, value, me, first, peer):
        slots[pl.ds(me, 1), :] = value
        mine = slots.at[pl.ds(me, 1)]
        out = [b_copy(mine, mine, first + k, peer(k + 1)) for k in range(3)]
        for copy in out:
            copy.start()
        return out

    def ordered(slots, count):
        total = slots[0:1, :]
        for i in range(1, count):
            total = total + slots[i : i + 1, :]
        return total

    def grad_chunk(n):
        cols = pl.ds(n * 256, 256)

        def body(sub, carry):
            at = pl.ds(pl.multiple_of(sub * SUB, 128), SUB)
            own_at = pl.ds(pl.multiple_of(y * QROWS + sub * SUB, 128), SUB)

            def outer(rows, values):
                return lax.dot_general(
                    rows.reshape(TOK, SUB), values, FIRST, preferred_element_type=F32
                )

            total = outer(cen[:, :, :, :, own_at], pre[:, cols])
            total = total + outer(err[:, :, :, :, own_at], lat[:, cols])
            for k in range(3):
                total = total + outer(cen_y[k, :, :, :, :, at], pre_y[k, :, cols])
                total = total + outer(err_y[k, :, :, :, :, at], lat_y[k, :, cols])
            tmp[pl.ds(pl.multiple_of(sub * SUB, 128), SUB), :] = total
            return carry

        lax.fori_loop(0, 3, body, 0)
        theirs = pl.ds(pl.multiple_of((1 - zl) * OWN, 64), OWN)
        ours = pl.ds(pl.multiple_of(zl * OWN, 64), OWN)
        zsend[:, cols] = tmp[theirs, :].astype(BF16)
        copy = remote(zsend.at[:, cols], zrecv.at[:, cols], z_s.at[n], z_r.at[n], zpart)
        copy.start()
        own_grad[:, cols] = tmp[ours, :]
        return copy

    send_onward(0)
    send_near(2)
    err_part[2]()
    send_onward(1)
    send_near(3)
    cen_part[3]()
    err_part[3]()
    for copy in lat_out:
        copy.wait()
    for copy in bias:
        copy.wait()
    ezr[pl.ds(zl, 1), :] = ordered(esr, 4)
    mine = ezr.at[pl.ds(zl, 1)]
    enc = b_copy(mine, mine, 4, zpart)
    enc.start()
    bias = dec_stage(dx_r, ordered(dcore, 2), x, 5, xpeer)

    zout = []
    for n in range(4):
        if n in (1, 2):
            send_onward(n + 1)
        for copy in onward[n]:
            copy.wait()
        zout.append(grad_chunk(n))
        if n == 0:
            for copy in bias:
                copy.wait()
            bias = dec_stage(dz_r, ordered(dx_r, 4), z, 8, zpeer)
        elif n == 1:
            for copy in bias:
                copy.wait()
            bias = dec_stage(dy_r, ordered(dz_r, 4), y, 11, ypeer)
    enc.wait()
    enc_out[...] = ezr[...]
    for copy in bias:
        copy.wait()
    dec_out[...] = ordered(dy_r, 4)
    for copy in zout:
        copy.wait()


def write_out(stream, own_grad, their_grad, enc, dec, stream_out, wgrad, enc_out, dec_out):
    zl = lax.axis_index("dp") % 2
    here = pl.ds(pl.multiple_of(zl * LAT, LAT), LAT)
    there = pl.ds(pl.multiple_of((1 - zl) * LAT, LAT), LAT)
    wgrad[:, here] = own_grad[...]
    wgrad[:, there] = their_grad[...].astype(F32)

    @pl.when(pl.program_id(0) == 0)
    def _():
        stream_out[...] = stream[...]
        enc_out[pl.ds(0, LAT)] = enc[0, :]
        enc_out[pl.ds(LAT, LAT)] = enc[1, :]
        dec_out[...] = dec[0, :]


def per_device(attn_values, out_proj, post_gain, residual, sae_weight, enc_bias, dec_bias):
    vmem = pl.BlockSpec(memory_space=pltpu.VMEM)
    hbm = pl.BlockSpec(memory_space=pl.ANY)
    block = (4, 4, ROWS, D)
    dma = pltpu.SemaphoreType.DMA
    parts = pl.pallas_call(
        kernel,
        out_shape=(
            jax.ShapeDtypeStruct((ROWS, D), BF16),
            jax.ShapeDtypeStruct((OWN, LAT), F32),
            jax.ShapeDtypeStruct((OWN, LAT), BF16),
            jax.ShapeDtypeStruct((2, LAT), F32),
            jax.ShapeDtypeStruct((1, D), F32),
        ),
        in_specs=[vmem, vmem, vmem, vmem, hbm, vmem, vmem],
        out_specs=(vmem, vmem, vmem, vmem, vmem),
        scratch_shapes=[
            pltpu.VMEM((D, LAT), BF16),
            pltpu.VMEM((2,) + block, BF16),
            pltpu.VMEM((2,) + block, BF16),
            pltpu.VMEM((3, 2, 4, 4, ROWS, QROWS), BF16),
            pltpu.VMEM((3, 2, 4, 4, ROWS, QROWS), BF16),
            pltpu.VMEM((TOK, LAT), F32),
            pltpu.VMEM((TOK, LAT), BF16),
            pltpu.VMEM((TOK, LAT), BF16),
            pltpu.VMEM((3, TOK, LAT), BF16),
            pltpu.VMEM((3, TOK, LAT), BF16),
            pltpu.VMEM(block, BF16),
            pltpu.VMEM(block, F32),
            pltpu.VMEM(block, BF16),
            pltpu.VMEM((7, ROWS, D), BF16),
            pltpu.VMEM((3, 4, ROWS, HALF), BF16),
            pltpu.VMEM((3, 4, ROWS, HALF), BF16),
            pltpu.VMEM((4, ROWS, HALF), BF16),
            pltpu.VMEM((4, ROWS, HALF), BF16),
            pltpu.VMEM((3, ROWS, HALF), BF16),
            pltpu.VMEM((3, ROWS, HALF), BF16),
            pltpu.VMEM((OWN, LAT), BF16),
            pltpu.VMEM((QROWS, 256), F32),
            pltpu.VMEM((16, LAT), BF16),
            pltpu.VMEM((4, LAT), F32),
            pltpu.VMEM((2, LAT), F32),
            pltpu.VMEM((2, D), F32),
            pltpu.VMEM((4, D), F32),
            pltpu.VMEM((4, D), F32),
            pltpu.VMEM((4, D), F32),
            dma, dma, dma, dma((7,)), dma((7,)), dma((4, 21)), dma((4, 21)),
            dma((2,)), dma((2,)), dma((6,)), dma((6,)), dma((6,)), dma((6,)),
            dma((2, 3)), dma((2, 3)), dma((3,)), dma((3,)), dma((4, 4)), dma((4, 4)),
            dma((4,)), dma((4,)), dma((14,)), dma((14,)),
        ],
        compiler_params=pltpu.CompilerParams(
            collective_id=0, has_side_effects=True, vmem_limit_bytes=63 * 2**20
        ),
        cost_estimate=pl.CostEstimate(
            flops=25 * 10**9, bytes_accessed=20 * 10**6, transcendentals=0
        ),
    )(
        attn_values.reshape(2, 4, 2, ROWS, 256),
        out_proj, post_gain, residual, sae_weight, enc_bias, dec_bias,
    )
    steps = 6

    def fixed(*shape):
        return pl.BlockSpec(shape, lambda i: (0,) * len(shape))

    def rows(width):
        return pl.BlockSpec((OWN // steps, width), lambda i: (i, 0))

    return tuple(
        pl.pallas_call(
            write_out,
            grid=(steps,),
            out_shape=(
                jax.ShapeDtypeStruct((ROWS, D), BF16),
                jax.ShapeDtypeStruct((OWN, 2 * LAT), F32),
                jax.ShapeDtypeStruct((2 * LAT,), F32),
                jax.ShapeDtypeStruct((D,), F32),
            ),
            in_specs=[fixed(ROWS, D), rows(LAT), rows(LAT), fixed(2, LAT), fixed(1, D)],
            out_specs=(fixed(ROWS, D), rows(2 * LAT), fixed(2 * LAT), fixed(D)),
        )(*parts)
    )


def solution(mesh):
    return jax.shard_map(
        per_device,
        mesh=mesh,
        in_specs=(
            P("dp", "mp"),
            P("mp", None),
            P(),
            P(("dp", "mp"), None),
            P(None, "mp"),
            P("mp"),
            P(),
        ),
        out_specs=(P(("dp", "mp"), None), P("dp", "mp"), P("mp"), P()),
        check_vma=False,
    )
```

time: 233 us -> 188 us (0.81)
  Pallas kernels: 218 us -> 187 us
  local copies, waits for them, and re-layouts: 12 us -> 0 us
    pallas_call x1, Pallas kernels: 218 us -> 181 us  [per_device(): pl.pallas_call(kernel, out_shape=(jax.ShapeDtypeStruct((ROWS, D), BF16),...]
    unnamed x3 -> x0, local copies, waits for them, and re-layouts: 7.97 us -> none
    pallas_call x0 -> x1, Pallas kernels: none -> 5.82 us  [per_device(): pl.pallas_call(write_out, grid=(steps,), out_shape=(jax.ShapeDtypeStruct(...]
    reshape x3 -> x0, local copies, waits for them, and re-layouts: 4 us -> none  [the longest x1 1.35 us: per_device(): post_gain.reshape(1, D)]
where the time goes in v2:
time: 188 us
  Pallas kernels  187 us (99%)
    pallas_call x1, Pallas kernels, per_device(): pl.pallas_call(kernel, out_shape=(jax.ShapeDtypeStruct((ROWS, D), BF16),...  181 us
    pallas_call x1, Pallas kernels, per_device(): pl.pallas_call(write_out, grid=(steps,), out_shape=(jax.ShapeDtypeStruct(...  5.82 us

profile of v2, /device:TPU:0, one launch (start us, length us, event | category | flops | bytes accessed | tf_op | source)
XLA Modules:
  0.0 187.6 jit_solution(11881908763966871417)
XLA Ops:
  0.6 181.2 %shard_map.102 = (bf16[16,4608]{1,0:T(8,128)(2,1)}, f32[576,1024]{1,0:T(8,128)}, bf16[576,1024]{1,0:T(8,128)(2,1)}, f32[2,1024]{1,0:T(2,128)}, f32[1,4608]{1,0:T(1,128)}) custom-call(bf16[2,4,2,16,256]{4,3,2,1,0:T(8,128)(2,1)} %bitcast.1, bf16[256,4608]{1,0:T(8,128)(2,1)} %oproj.1, f32[4608]{0:T(1024)} %gain.1, bf16[16,4608]{1,0:T(8,128)(2,1)} %resid.1, ...), custom_call_target="tpu_custom_call" | custom-call | flops 24999999488 | bytes 20000000 | tf_op jit(solution)/shard_map/pallas_call | solution.py:483
  181.8 5.8 %shard_map.103 = (bf16[16,4608]{1,0:T(8,128)(2,1)}, f32[576,2048]{1,0:T(8,128)}, f32[2048]{0:T(1024)}, f32[4608]{0:T(1024)}) custom-call(bf16[16,4608]{1,0:T(8,128)(2,1)} %get-tuple-element.9.stream, f32[576,1024]{1,0:T(8,128)} %get-tuple-element.10.own_grad, bf16[576,1024]{1,0:T(8,128)(2,1)} %get-tuple-element.11.their_grad, ...), custom_call_target="tpu_custom_call" | custom-call | tf_op jit(solution)/shard_map/pallas_call | solution.py:548

commit v3 on v2

v3 whole, which is shorter than its diff:
```python
import math

import jax
import jax.numpy as jnp
from jax import lax
from jax.experimental import pallas as pl
from jax.experimental.pallas import tpu as pltpu
from jax.sharding import PartitionSpec as P

SPARSITY = 0.5
D = 4608
LAT = 1024
HALF = D // 2
PART = HALF // 2
ROWS = 16
TOK = 512
BATCH = 256
QROWS = D // 4
SUB = QROWS // 3
OWN = QROWS // 2
TOKENS = 2048
SCALE = 1.0 / math.sqrt(TOKENS)
F32 = jnp.float32
BF16 = jnp.bfloat16
CUTS = (pl.ds(0, PART), pl.ds(PART, PART))
LAST = (((1,), (1,)), ((), ()))
FIRST = (((0,), (0,)), ((), ()))


def kernel(
    attn, oproj, gain, resid, w_hbm, ebias, dbias,
    stream, own_grad, zrecv, enc_out, dec_out,
    w_v, cen, err, cen_y, err_y, pos, lat, pre, lat_y, pre_y,
    rsend, rown, rrecv, p1r2,
    rz, rx, s2a, s2b, r2a, r2b,
    zsend, tmp, res2, str2, att, ssq, gain2, shift2,
    es3, esr, ezr, dcore, dx_r, dz_r, dy_r,
    w_sem, rs_s, rs_r, st_s, st_r, ss_s, ss_r, p1_s, p1_r, p2_s, p2_r, ag_s, ag_r,
    rc_s, rc_r, r1_s, r1_r, r2_s, r2_r,
    yp_s, yp_r, yl_s, yl_r, y_s, y_r, z_s, z_r, b_s, b_r,
):
    dp, mp = lax.axis_index("dp"), lax.axis_index("mp")
    y, zl = dp // 2, dp % 2
    zh, x, c = mp // 8, (mp // 2) % 4, mp % 2
    z = zh * 2 + zl

    def dev(x_, y_, z_, c_):
        return (y_ * 2 + z_ % 2, (z_ // 2) * 8 + x_ * 2 + c_)

    core = dev(x, y, z, 1 - c)

    def xpeer(k):
        return dev((x + k) % 4, y, z, c)

    def zpeer(k):
        return dev(x, y, (z + k) % 4, c)

    def ypeer(k):
        return dev(x, (y + k) % 4, z, c)

    zpart = dev(x, y, zh * 2 + 1 - zl, c)

    def far(j):
        return dev((x + j % 4) % 4, y, ((zh + j // 4) % 2) * 2 + zl, c)

    def remote(src, dst, ssem, rsem, to):
        return pltpu.make_async_remote_copy(
            src_ref=src, dst_ref=dst, send_sem=ssem, recv_sem=rsem,
            device_id=to, device_id_type=pl.DeviceIdType.MESH,
        )

    w_copy = pltpu.make_async_copy(
        w_hbm.at[:, pl.ds(pl.multiple_of(zl * LAT, LAT), LAT)], w_v, w_sem
    )
    w_copy.start()

    barrier = pltpu.get_barrier_semaphore()
    partners = [core]
    for k in (1, 2, 3):
        partners += [xpeer(k), zpeer(k), ypeer(k), far(4 + k)]
    for to in partners:
        pl.semaphore_signal(barrier, inc=1, device_id=to, device_id_type=pl.DeviceIdType.MESH)
    pl.semaphore_wait(barrier, len(partners))

    def half(which, at=0, width=HALF):
        return pl.ds(pl.multiple_of(which * HALF + at, 128), width)

    mine_cols, their_cols = half(c), half(1 - c)

    res_out = remote(resid.at[:, their_cols], res2.at[c], rs_s, rs_r, core)
    res_out.start()
    res2[c] = resid[:, mine_cols]
    row = gain[...].reshape(1, D)
    gain2[...] = jnp.where(c == 0, row[:, :HALF], row[:, HALF:])
    row = dbias[...].reshape(1, D)
    shift2[...] = jnp.where(c == 0, row[:, :HALF], row[:, HALF:])

    def proj(b, which, j):
        rows = attn[:, :, b].reshape(128, 256)
        part = jnp.dot(rows, oproj[:, half(which, j * 768, 768)], preferred_element_type=F32)
        return pl.ds(pl.multiple_of(j * 768, 768), 768), part.reshape(2, 4, ROWS, 768)

    p1, p2 = [], [[], []]
    for b in (0, 1):

        def peer_proj(j, carry, b=b):
            cols, part = proj(b, 1 - c, j)
            rsend[b, pl.ds(0, 2), :, :, cols] = part.astype(BF16)
            return carry

        lax.fori_loop(0, 3, peer_proj, 0)
        two = pl.ds(0, 2)
        p1.append(remote(rsend.at[b, two], rrecv.at[b, two], p1_s.at[b], p1_r.at[b], core))
        p1[b].start()
    for b in (0, 1):

        def own_proj(j, carry, b=b):
            cols, part = proj(b, c, j)
            rown[b, pl.ds(0, 2), :, :, cols] = part
            return carry

        lax.fori_loop(0, 3, own_proj, 0)
        p1[b].wait()

        def add_proj(j, carry, b=b):
            total = rown[b, j // 4, j % 4] + rrecv[b, j // 4, j % 4].astype(F32)
            rown[b, j // 4, j % 4] = total
            rrecv[b, j // 4, j % 4] = total.astype(BF16)
            return carry

        lax.fori_loop(0, 8, add_proj, 0)
        for j in range(1, 8):
            p2[b].append(
                remote(
                    rrecv.at[b, (zh + j // 4) % 2, (x + j % 4) % 4], p1r2.at[b, j - 1],
                    p2_s.at[b, j - 1], p2_r.at[b, j - 1], far(j),
                )
            )
            p2[b][-1].start()

    def gather(at, start, cut, width, phase):
        left = pl.ds(start, cut)
        right = pl.ds(start + cut, width - cut)
        if not isinstance(start, int):
            left = pl.ds(pl.multiple_of(start, 128), cut)
            right = pl.ds(pl.multiple_of(start + cut, 128), width - cut)
        every = slice(None)

        def copy(ref, i, to):
            return remote(ref, ref, ag_s.at[phase, i], ag_r.at[phase, i], to)

        first, second, third = [], [], []
        for k in (1, 2, 3):
            first.append(copy(at(z, x, left), k, xpeer(k)))
            first.append(copy(at(z, x, right), 3 + k, zpeer(k)))
            second.append(copy(at(z, every, left), 6 + k, zpeer(k)))
            second.append(copy(at(every, x, right), 9 + k, xpeer(k)))
        third.append(copy(at(z, every, left), 13, core))
        third.append(copy(at(every, x, right), 14, core))
        for k in (1, 2, 3):
            third.append(copy(at((z + 4 - k) % 4, every, left), 14 + k, core))
            third.append(copy(at(every, (x + 4 - k) % 4, right), 17 + k, core))

        def begin():
            for one in first:
                one.start()

        def spread():
            for one in first:
                one.wait()
            for one in second + third[:2]:
                one.start()

        def share():
            for came, one in zip(second, third[2:]):
                came.wait()
                one.start()

        def end():
            for one in third:
                one.wait()

        return begin, spread, share, end, third

    def rows_of(buf, b, phase):
        return gather(
            lambda z_, x_, cols: buf.at[b, z_, x_, :, cols], c * HALF, PART, HALF, phase
        )

    active = c == y // 2

    def part_of(buf, buf_y, b, phase):
        start, spread, share, end, third = gather(
            lambda z_, x_, cols: buf_y.at[:, b, z_, x_, :, cols], 0, 640, QROWS, 4 + phase
        )

        def piece(k, i):
            to = dev(x, (y + k) % 4, z, c)
            cols = pl.ds(pl.multiple_of(((y + k) % 4) * QROWS, 128), QROWS)
            return remote(
                buf.at[b, z, x, :, cols], buf_y.at[k - 1, b, z, x],
                yp_s.at[phase, i], yp_r.at[phase, k - 1], to,
            )

        def each(act):
            for i in (0, 1):
                k = (2 * c + i + 4 - y) % 4

                @pl.when(k > 0)
                def _(k=k, i=i):
                    act(piece(k, i))

        def send():
            each(lambda copy: copy.start())

        def begin():
            each(lambda copy: copy.wait_send())

            @pl.when(active)
            def _():
                for k in (1, 2, 3):
                    piece(k, 0).wait_recv()
                start()

        def when_active(step):
            def run():
                pl.when(active)(step)

            return run

        def finish():
            @pl.when(active)
            def _():
                for copy in third:
                    copy.wait_send()

            @pl.when(jnp.logical_not(active))
            def _():
                for copy in third:
                    copy.wait_recv()

        return send, begin, when_active(spread), when_active(share), finish

    squares = []

    def sum_squares(b):
        for copy in p2[b]:
            copy.wait()
        total = rown[b, zh, x]
        for j in range(7):
            total = total + p1r2[b, j].astype(F32)
        att[b] = total
        own_sq = jnp.sum(total * total, axis=-1, keepdims=True)
        ssq[b, c] = jnp.broadcast_to(own_sq, (ROWS, 128))
        mine = ssq.at[b, c]
        squares.append(remote(mine, mine, ss_s.at[b], ss_r.at[b], core))
        squares[b].start()

    def norm(b):
        squares[b].wait()
        mean_sq = (ssq[b, 0] + ssq[b, 1])[:, 0:1] * (1.0 / D)
        normed = att[b] * lax.rsqrt(mean_sq + 1e-06) * gain2[...]
        rows = (res2[b].astype(F32) + normed).astype(BF16)
        str2[b] = rows
        cen[b, z, x, :, mine_cols] = (rows.astype(F32) - shift2[...]).astype(BF16)

    cen_rows = [rows_of(cen, b, b) for b in (0, 1)]
    err_rows = [rows_of(err, b, 2 + b) for b in (0, 1)]
    cen_part = [part_of(cen, cen_y, b, b) for b in (0, 1)]
    err_part = [part_of(err, err_y, b, 2 + b) for b in (0, 1)]

    sum_squares(0)
    res_out.wait()
    norm(0)
    cen_rows[0][0]()
    cen_part[0][0]()
    sum_squares(1)
    norm(1)
    cen_rows[1][0]()
    cen_part[1][0]()
    stream_out = remote(str2.at[1 - c], stream.at[:, mine_cols], st_s, st_r, core)
    stream_out.start()
    stream[:, mine_cols] = str2[c]

    cen_rows[0][1]()
    cen_rows[1][1]()
    cen_part[0][1]()
    cen_part[1][1]()
    row = ebias[...].reshape(2, LAT)
    ezr[0:1, :] = jnp.where(zl == 0, row[0:1], row[1:2])
    w_copy.wait()

    def encode(b):
        def body(n, carry):
            cols = pl.ds(pl.multiple_of(n * 256, 256), 256)
            act = jnp.dot(
                cen[b].reshape(BATCH, D), w_v[:, cols], preferred_element_type=F32
            )
            act = jnp.maximum(act + ezr[0:1, cols], 0.0)
            pos[b, :, cols] = act
            lat[b, :, cols] = (act * act).astype(BF16)
            return carry

        lax.fori_loop(0, 4, body, 0)

    def round_y(own, got, cols, s_sem, r_sem):
        top, low = pl.ds(0, BATCH // 2), pl.ds(BATCH // 2, BATCH // 2)
        near = [
            remote(own.at[:, cols], got(0).at[:, cols], s_sem.at[0], r_sem.at[0], ypeer(1)),
            remote(own.at[:, cols], got(2).at[:, cols], s_sem.at[1], r_sem.at[1], ypeer(3)),
        ]
        on = [
            remote(
                got(0).at[top, cols], got(1).at[top, cols], s_sem.at[2], r_sem.at[2], ypeer(1)
            ),
            remote(
                got(2).at[low, cols], got(1).at[low, cols], s_sem.at[3], r_sem.at[3], ypeer(3)
            ),
        ]

        def begin():
            for copy in near:
                copy.start()

        def onward():
            for copy, came in zip(on, near):
                came.wait()
                copy.start()

        def end():
            for copy in on:
                copy.wait()

        return begin, onward, end

    lat_round = [
        round_y(
            lat.at[b], lambda k, b=b: lat_y.at[k, b], pl.ds(0, LAT), yl_s.at[b], yl_r.at[b]
        )
        for b in (0, 1)
    ]

    def decode(b, which, j):
        rows = half(which, j * 256, 256)
        part = lax.dot_general(lat[b], w_v[rows, :], LAST, preferred_element_type=F32)
        return pl.ds(pl.multiple_of(j * 256, 256), 256), part.reshape(4, 4, ROWS, 256)

    rc, r1, r2 = [], [[], []], [[], []]

    def decode_peer(b):
        def body(j, carry):
            cols, part = decode(b, 1 - c, j)
            rsend[b, :, :, :, cols] = part.astype(BF16)
            return carry

        lax.fori_loop(0, 9, body, 0)
        rc.append(remote(rsend.at[b], rrecv.at[b], rc_s.at[b], rc_r.at[b], core))
        rc[b].start()

    def decode_own(b):
        def body(j, carry):
            cols, part = decode(b, c, j)
            rown[b, :, :, :, cols] = part
            return carry

        lax.fori_loop(0, 9, body, 0)

    def recon_first(b):
        rc[b].wait()

        def body(j, carry):
            total = rown[b, j // 4, j % 4] + rrecv[b, j // 4, j % 4].astype(F32)
            rown[b, j // 4, j % 4] = total
            rrecv[b, j // 4, j % 4] = total.astype(BF16)
            return carry

        lax.fori_loop(0, 16, body, 0)
        for k in (1, 2, 3):
            for h in (0, 1):
                if h == 0:
                    src, dst, to = rrecv.at[b, (z + k) % 4, :, :, CUTS[0]], rz, zpeer(k)
                else:
                    src, dst, to = rrecv.at[b, :, (x + k) % 4, :, CUTS[1]], rx, xpeer(k)
                i = 2 * k - 2 + h
                r1[b].append(remote(src, dst.at[b, k - 1], r1_s.at[b, i], r1_r.at[b, i], to))
                r1[b][-1].start()

    def recon_second(b):
        for copy in r1[b]:
            copy.wait()
        for i in range(4):
            total = rown[b, z, i, :, CUTS[0]]
            for k in range(3):
                total = total + rz[b, k, i].astype(F32)
            rown[b, z, i, :, CUTS[0]] = total
            s2a[b, i] = total.astype(BF16)
            total = rown[b, i, x, :, CUTS[1]]
            for k in range(3):
                total = total + rx[b, k, i].astype(F32)
            rown[b, i, x, :, CUTS[1]] = total
            s2b[b, i] = total.astype(BF16)
        for k in (1, 2, 3):
            for h in (0, 1):
                if h == 0:
                    src, dst, to = s2a.at[b, (x + k) % 4], r2a, xpeer(k)
                else:
                    src, dst, to = s2b.at[b, (z + k) % 4], r2b, zpeer(k)
                i = 2 * k - 2 + h
                r2[b].append(remote(src, dst.at[b, k - 1], r2_s.at[b, i], r2_r.at[b, i], to))
                r2[b][-1].start()

    def error(b):
        for copy in r2[b]:
            copy.wait()
        for h in (0, 1):
            total = rown[b, z, x, :, CUTS[h]]
            for k in range(3):
                total = total + (r2a, r2b)[h][b, k].astype(F32)
            grad = total + shift2[:, CUTS[h]] - str2[b, :, CUTS[h]].astype(F32)
            grad = (grad * SCALE).astype(BF16)
            cols = half(c, h * PART, PART)
            err[b, z, x, :, cols] = grad
            sums = jnp.sum(grad.astype(F32), axis=0, keepdims=True)
            dcore[pl.ds(c, 1), cols] = dcore[pl.ds(c, 1), cols] + sums

    cen_rows[0][2]()
    cen_rows[0][3]()
    encode(0)
    lat_round[0][0]()
    cen_part[0][2]()
    decode_peer(0)
    decode_own(0)
    cen_rows[1][2]()
    recon_first(0)
    cen_rows[1][3]()
    encode(1)
    lat_round[1][0]()
    decode_peer(1)
    decode_own(1)
    recon_first(1)
    cen_part[1][2]()
    lat_round[0][1]()
    dcore[pl.ds(c, 1), :] = jnp.zeros((1, D), F32)
    recon_second(0)
    cen_part[0][3]()
    recon_second(1)
    error(0)
    err_rows[0][0]()
    err_part[0][0]()
    error(1)
    err_rows[1][0]()
    err_part[1][0]()
    cen_part[1][3]()
    err_rows[0][1]()
    err_rows[1][1]()
    lat_round[1][1]()
    err_part[0][1]()
    err_part[1][1]()
    err_rows[0][2]()
    err_rows[0][3]()

    def back(b):
        def body(n, carry):
            cols = pl.ds(pl.multiple_of(n * 256, 256), 256)
            grad = jnp.dot(
                err[b].reshape(BATCH, D), w_v[:, cols], preferred_element_type=F32
            )
            grad = ((grad + SPARSITY * SCALE) * (2.0 * pos[b, :, cols])).astype(BF16)
            pre[b, :, cols] = grad
            sums = jnp.sum(grad.astype(F32), axis=0, keepdims=True)
            if b == 1:
                sums = sums + esr[pl.ds(y, 1), cols]
            esr[pl.ds(y, 1), cols] = sums
            return carry

        lax.fori_loop(0, 4, body, 0)

    pre_round = [
        [
            round_y(
                pre.at[b], lambda k, b=b: pre_y.at[k, b], pl.ds(n * 256, 256),
                y_s.at[b, n], y_r.at[b, n],
            )
            for n in range(4)
        ]
        for b in (0, 1)
    ]
    back(0)
    for n in range(4):
        pre_round[0][n][0]()
    err_part[0][2]()
    err_rows[1][2]()
    err_rows[1][3]()
    back(1)
    pre_round[1][0][0]()
    pre_round[1][1][0]()
    err_part[1][2]()
    pre_round[0][0][1]()
    pre_round[0][1][1]()

    own_sum = esr[pl.ds(y, 1), :]
    high = own_sum.astype(BF16)
    rest = own_sum - high.astype(F32)
    mid = rest.astype(BF16)
    bottom = (rest - mid.astype(F32)).astype(BF16)
    es3[...] = jnp.concatenate([high, mid, bottom, jnp.zeros((13, LAT), BF16)], axis=0)

    def b_copy(src, dst, i, to):
        return remote(src, dst, b_s.at[i], b_r.at[i], to)

    bias = []
    mine = esr.at[pl.ds(y, 1)]
    for k in (1, 2, 3):
        bias.append(b_copy(mine, mine, k - 1, ypeer(k)))
    for copy in bias:
        copy.start()

    def project(j, carry):
        cols = pl.ds(pl.multiple_of(j * 512, 512), 512)
        part = lax.dot_general(es3[...], w_v[cols, :], LAST, preferred_element_type=F32)
        dcore[pl.ds(c, 1), cols] = dcore[pl.ds(c, 1), cols] - jnp.sum(part, axis=0, keepdims=True)
        return carry

    lax.fori_loop(0, 9, project, 0)
    mine = dcore.at[pl.ds(c, 1)]
    bias.append(b_copy(mine, mine, 3, core))
    bias[-1].start()

    def dec_stage(slots, value, me, first, peer):
        slots[pl.ds(me, 1), :] = value
        mine = slots.at[pl.ds(me, 1)]
        out = [b_copy(mine, mine, first + k, peer(k + 1)) for k in range(3)]
        for copy in out:
            copy.start()
        return out

    def ordered(slots, count):
        total = slots[0:1, :]
        for i in range(1, count):
            total = total + slots[i : i + 1, :]
        return total

    def grad_chunk(n):
        cols = pl.ds(n * 256, 256)

        def body(sub, carry):
            at = pl.ds(pl.multiple_of(sub * SUB, 128), SUB)
            own_at = pl.ds(pl.multiple_of(y * QROWS + sub * SUB, 128), SUB)

            def outer(rows, values):
                return lax.dot_general(
                    rows.reshape(TOK, SUB), values.reshape(TOK, 256), FIRST,
                    preferred_element_type=F32,
                )

            total = outer(cen[:, :, :, :, own_at], pre[:, :, cols])
            total = total + outer(err[:, :, :, :, own_at], lat[:, :, cols])
            for k in range(3):
                total = total + outer(cen_y[k, :, :, :, :, at], pre_y[k, :, :, cols])
                total = total + outer(err_y[k, :, :, :, :, at], lat_y[k, :, :, cols])
            tmp[pl.ds(pl.multiple_of(sub * SUB, 128), SUB), :] = total
            return carry

        lax.fori_loop(0, 3, body, 0)
        theirs = pl.ds(pl.multiple_of((1 - zl) * OWN, 64), OWN)
        ours = pl.ds(pl.multiple_of(zl * OWN, 64), OWN)
        zsend[:, cols] = tmp[theirs, :].astype(BF16)
        copy = remote(zsend.at[:, cols], zrecv.at[:, cols], z_s.at[n], z_r.at[n], zpart)
        copy.start()
        own_grad[:, cols] = tmp[ours, :]
        return copy

    pre_round[0][2][1]()
    pre_round[0][3][1]()
    for b in (0, 1):
        cen_part[b][4]()
    err_part[0][3]()
    pre_round[1][0][1]()
    pre_round[1][2][0]()
    err_part[1][3]()
    for copy in bias:
        copy.wait()
    ezr[pl.ds(zl, 1), :] = ordered(esr, 4)
    mine = ezr.at[pl.ds(zl, 1)]
    enc = b_copy(mine, mine, 4, zpart)
    enc.start()
    bias = dec_stage(dx_r, ordered(dcore, 2), x, 5, xpeer)
    pre_round[1][1][1]()
    pre_round[1][3][0]()
    for b in (0, 1):
        lat_round[b][2]()
        err_part[b][4]()

    zout = []
    for n in range(4):
        for b in (0, 1):
            pre_round[b][n][2]()
        zout.append(grad_chunk(n))
        if n < 2:
            pre_round[1][n + 2][1]()
        if n == 0:
            for copy in bias:
                copy.wait()
            bias = dec_stage(dz_r, ordered(dx_r, 4), z, 8, zpeer)
        elif n == 1:
            for copy in bias:
                copy.wait()
            bias = dec_stage(dy_r, ordered(dz_r, 4), y, 11, ypeer)
    stream_out.wait()
    enc.wait()
    enc_out[...] = ezr[...]
    for copy in bias:
        copy.wait()
    dec_out[...] = ordered(dy_r, 4)
    for copy in zout:
        copy.wait()


def write_out(stream, own_grad, their_grad, enc, dec, stream_out, wgrad, enc_out, dec_out):
    zl = lax.axis_index("dp") % 2
    here = pl.ds(pl.multiple_of(zl * LAT, LAT), LAT)
    there = pl.ds(pl.multiple_of((1 - zl) * LAT, LAT), LAT)
    wgrad[:, here] = own_grad[...]
    wgrad[:, there] = their_grad[...].astype(F32)

    @pl.when(pl.program_id(0) == 0)
    def _():
        stream_out[...] = stream[...]
        enc_out[pl.ds(0, LAT)] = enc[0, :]
        enc_out[pl.ds(LAT, LAT)] = enc[1, :]
        dec_out[...] = dec[0, :]


def per_device(attn_values, out_proj, post_gain, residual, sae_weight, enc_bias, dec_bias):
    vmem = pl.BlockSpec(memory_space=pltpu.VMEM)
    hbm = pl.BlockSpec(memory_space=pl.ANY)
    block = (2, 4, 4, ROWS, HALF)
    dma = pltpu.SemaphoreType.DMA
    parts = pl.pallas_call(
        kernel,
        out_shape=(
            jax.ShapeDtypeStruct((ROWS, D), BF16),
            jax.ShapeDtypeStruct((OWN, LAT), F32),
            jax.ShapeDtypeStruct((OWN, LAT), BF16),
            jax.ShapeDtypeStruct((2, LAT), F32),
            jax.ShapeDtypeStruct((1, D), F32),
        ),
        in_specs=[vmem, vmem, vmem, vmem, hbm, vmem, vmem],
        out_specs=(vmem, vmem, vmem, vmem, vmem),
        scratch_shapes=[
            pltpu.VMEM((D, LAT), BF16),
            pltpu.VMEM((2, 4, 4, ROWS, D), BF16),
            pltpu.VMEM((2, 4, 4, ROWS, D), BF16),
            pltpu.VMEM((3, 2, 4, 4, ROWS, QROWS), BF16),
            pltpu.VMEM((3, 2, 4, 4, ROWS, QROWS), BF16),
            pltpu.VMEM((2, BATCH, LAT), F32),
            pltpu.VMEM((2, BATCH, LAT), BF16),
            pltpu.VMEM((2, BATCH, LAT), BF16),
            pltpu.VMEM((3, 2, BATCH, LAT), BF16),
            pltpu.VMEM((3, 2, BATCH, LAT), BF16),
            pltpu.VMEM(block, BF16),
            pltpu.VMEM(block, F32),
            pltpu.VMEM(block, BF16),
            pltpu.VMEM((2, 7, ROWS, HALF), BF16),
            pltpu.VMEM((2, 3, 4, ROWS, PART), BF16),
            pltpu.VMEM((2, 3, 4, ROWS, PART), BF16),
            pltpu.VMEM((2, 4, ROWS, PART), BF16),
            pltpu.VMEM((2, 4, ROWS, PART), BF16),
            pltpu.VMEM((2, 3, ROWS, PART), BF16),
            pltpu.VMEM((2, 3, ROWS, PART), BF16),
            pltpu.VMEM((OWN, LAT), BF16),
            pltpu.VMEM((QROWS, 256), F32),
            pltpu.VMEM((2, ROWS, HALF), BF16),
            pltpu.VMEM((2, ROWS, HALF), BF16),
            pltpu.VMEM((2, ROWS, HALF), F32),
            pltpu.VMEM((2, 2, ROWS, 128), F32),
            pltpu.VMEM((1, HALF), F32),
            pltpu.VMEM((1, HALF), F32),
            pltpu.VMEM((16, LAT), BF16),
            pltpu.VMEM((4, LAT), F32),
            pltpu.VMEM((2, LAT), F32),
            pltpu.VMEM((2, D), F32),
            pltpu.VMEM((4, D), F32),
            pltpu.VMEM((4, D), F32),
            pltpu.VMEM((4, D), F32),
            dma, dma, dma, dma, dma, dma((2,)), dma((2,)), dma((2,)), dma((2,)),
            dma((2, 7)), dma((2, 7)), dma((8, 21)), dma((8, 21)),
            dma((2,)), dma((2,)), dma((2, 6)), dma((2, 6)), dma((2, 6)), dma((2, 6)),
            dma((4, 2)), dma((4, 3)), dma((2, 4)), dma((2, 4)), dma((2, 4, 4)), dma((2, 4, 4)),
            dma((4,)), dma((4,)), dma((14,)), dma((14,)),
        ],
        compiler_params=pltpu.CompilerParams(
            collective_id=0, has_side_effects=True, vmem_limit_bytes=63 * 2**20
        ),
        cost_estimate=pl.CostEstimate(
            flops=25 * 10**9, bytes_accessed=20 * 10**6, transcendentals=0
        ),
    )(
        attn_values.reshape(2, 4, 2, ROWS, 256),
        out_proj, post_gain, residual, sae_weight, enc_bias, dec_bias,
    )
    steps = 6

    def fixed(*shape):
        return pl.BlockSpec(shape, lambda i: (0,) * len(shape))

    def rows(width):
        return pl.BlockSpec((OWN // steps, width), lambda i: (i, 0))

    return tuple(
        pl.pallas_call(
            write_out,
            grid=(steps,),
            out_shape=(
                jax.ShapeDtypeStruct((ROWS, D), BF16),
                jax.ShapeDtypeStruct((OWN, 2 * LAT), F32),
                jax.ShapeDtypeStruct((2 * LAT,), F32),
                jax.ShapeDtypeStruct((D,), F32),
            ),
            in_specs=[fixed(ROWS, D), rows(LAT), rows(LAT), fixed(2, LAT), fixed(1, D)],
            out_specs=(fixed(ROWS, D), rows(2 * LAT), fixed(2 * LAT), fixed(D)),
        )(*parts)
    )


def solution(mesh):
    return jax.shard_map(
        per_device,
        mesh=mesh,
        in_specs=(
            P("dp", "mp"),
            P("mp", None),
            P(),
            P(("dp", "mp"), None),
            P(None, "mp"),
            P("mp"),
            P(),
        ),
        out_specs=(P(("dp", "mp"), None), P("dp", "mp"), P("mp"), P()),
        check_vma=False,
    )
```

time: 188 us -> 174 us (0.926)
  Pallas kernels: 187 us -> 173 us
    pallas_call x1, Pallas kernels: 181 us -> 167 us  [per_device(): pl.pallas_call(kernel, out_shape=(jax.ShapeDtypeStruct((ROWS, D), BF16),...]
where the time goes in v3:
time: 174 us; the launch traced here: 173 us
  Pallas kernels  173 us (99%)
    pallas_call x1, Pallas kernels, per_device(): pl.pallas_call(kernel, out_shape=(jax.ShapeDtypeStruct((ROWS, D), BF16),...  167 us
    pallas_call x1, Pallas kernels, per_device(): pl.pallas_call(write_out, grid=(steps,), out_shape=(jax.ShapeDtypeStruct(...  5.82 us

profile of v3, /device:TPU:0, one launch (start us, length us, event | category | flops | bytes accessed | tf_op | source)
XLA Modules:
  0.0 173.4 jit_solution(6540411067326763659)
XLA Ops:
  0.6 166.9 %shard_map.102 = (bf16[16,4608]{1,0:T(8,128)(2,1)}, f32[576,1024]{1,0:T(8,128)}, bf16[576,1024]{1,0:T(8,128)(2,1)}, f32[2,1024]{1,0:T(2,128)}, f32[1,4608]{1,0:T(1,128)}) custom-call(bf16[2,4,2,16,256]{4,3,2,1,0:T(8,128)(2,1)} %bitcast.1, bf16[256,4608]{1,0:T(8,128)(2,1)} %oproj.1, f32[4608]{0:T(1024)} %gain.1, bf16[16,4608]{1,0:T(8,128)(2,1)} %resid.1, ...), custom_call_target="tpu_custom_call" | custom-call | flops 24999999488 | bytes 20000000 | tf_op jit(solution)/shard_map/pallas_call | solution.py:639
  167.6 5.8 %shard_map.103 = (bf16[16,4608]{1,0:T(8,128)(2,1)}, f32[576,2048]{1,0:T(8,128)}, f32[2048]{0:T(1024)}, f32[4608]{0:T(1024)}) custom-call(bf16[16,4608]{1,0:T(8,128)(2,1)} %get-tuple-element.9.stream, f32[576,1024]{1,0:T(8,128)} %get-tuple-element.10.own_grad, bf16[576,1024]{1,0:T(8,128)(2,1)} %get-tuple-element.11.their_grad, ...), custom_call_target="tpu_custom_call" | custom-call | tf_op jit(solution)/shard_map/pallas_call | solution.py:711

commit v4 on v3

--- a/solution.py
+++ b/solution.py
@@ -466,7 +466,7 @@
                 err[b].reshape(BATCH, D), w_v[:, cols], preferred_element_type=F32
             )
             grad = ((grad + SPARSITY * SCALE) * (2.0 * pos[b, :, cols])).astype(BF16)
-            pre[b, :, cols] = grad
+            pre[b, n] = grad
             sums = jnp.sum(grad.astype(F32), axis=0, keepdims=True)
             if b == 1:
                 sums = sums + esr[pl.ds(y, 1), cols]
@@ -478,7 +478,7 @@
     pre_round = [
         [
             round_y(
-                pre.at[b], lambda k, b=b: pre_y.at[k, b], pl.ds(n * 256, 256),
+                pre.at[b, n], lambda k, b=b, n=n: pre_y.at[k, b, n], pl.ds(0, 256),
                 y_s.at[b, n], y_r.at[b, n],
             )
             for n in range(4)
@@ -486,8 +486,8 @@
         for b in (0, 1)
     ]
     back(0)
-    for n in range(4):
-        pre_round[0][n][0]()
+    pre_round[0][0][0]()
+    pre_round[0][1][0]()
     err_part[0][2]()
     err_rows[1][2]()
     err_rows[1][3]()
@@ -521,11 +521,6 @@
         dcore[pl.ds(c, 1), cols] = dcore[pl.ds(c, 1), cols] - jnp.sum(part, axis=0, keepdims=True)
         return carry
 
-    lax.fori_loop(0, 9, project, 0)
-    mine = dcore.at[pl.ds(c, 1)]
-    bias.append(b_copy(mine, mine, 3, core))
-    bias[-1].start()
-
     def dec_stage(slots, value, me, first, peer):
         slots[pl.ds(me, 1), :] = value
         mine = slots.at[pl.ds(me, 1)]
@@ -553,10 +548,10 @@
                     preferred_element_type=F32,
                 )
 
-            total = outer(cen[:, :, :, :, own_at], pre[:, :, cols])
+            total = outer(cen[:, :, :, :, own_at], pre[:, n])
             total = total + outer(err[:, :, :, :, own_at], lat[:, :, cols])
             for k in range(3):
-                total = total + outer(cen_y[k, :, :, :, :, at], pre_y[k, :, :, cols])
+                total = total + outer(cen_y[k, :, :, :, :, at], pre_y[k, :, n])
                 total = total + outer(err_y[k, :, :, :, :, at], lat_y[k, :, :, cols])
             tmp[pl.ds(pl.multiple_of(sub * SUB, 128), SUB), :] = total
             return carry
@@ -564,30 +559,22 @@
         lax.fori_loop(0, 3, body, 0)
         theirs = pl.ds(pl.multiple_of((1 - zl) * OWN, 64), OWN)
         ours = pl.ds(pl.multiple_of(zl * OWN, 64), OWN)
-        zsend[:, cols] = tmp[theirs, :].astype(BF16)
-        copy = remote(zsend.at[:, cols], zrecv.at[:, cols], z_s.at[n], z_r.at[n], zpart)
+        zsend[n] = tmp[theirs, :].astype(BF16)
+        copy = remote(zsend.at[n], zrecv.at[n], z_s.at[n], z_r.at[n], zpart)
         copy.start()
         own_grad[:, cols] = tmp[ours, :]
         return copy
 
-    pre_round[0][2][1]()
-    pre_round[0][3][1]()
+    pre_round[1][0][1]()
+    pre_round[0][2][0]()
+    pre_round[1][2][0]()
+    err_part[0][3]()
+    pre_round[1][1][1]()
+    pre_round[0][3][0]()
+    pre_round[1][3][0]()
+    err_part[1][3]()
     for b in (0, 1):
         cen_part[b][4]()
-    err_part[0][3]()
-    pre_round[1][0][1]()
-    pre_round[1][2][0]()
-    err_part[1][3]()
-    for copy in bias:
-        copy.wait()
-    ezr[pl.ds(zl, 1), :] = ordered(esr, 4)
-    mine = ezr.at[pl.ds(zl, 1)]
-    enc = b_copy(mine, mine, 4, zpart)
-    enc.start()
-    bias = dec_stage(dx_r, ordered(dcore, 2), x, 5, xpeer)
-    pre_round[1][1][1]()
-    pre_round[1][3][0]()
-    for b in (0, 1):
         lat_round[b][2]()
         err_part[b][4]()
 
@@ -597,14 +584,24 @@
             pre_round[b][n][2]()
         zout.append(grad_chunk(n))
         if n < 2:
-            pre_round[1][n + 2][1]()
+            for b in (0, 1):
+                pre_round[b][n + 2][1]()
+        for copy in bias:
+            copy.wait()
         if n == 0:
-            for copy in bias:
-                copy.wait()
+            ezr[pl.ds(zl, 1), :] = ordered(esr, 4)
+            mine = ezr.at[pl.ds(zl, 1)]
+            enc = b_copy(mine, mine, 4, zpart)
+            enc.start()
+            lax.fori_loop(0, 9, project, 0)
+            mine = dcore.at[pl.ds(c, 1)]
+            bias = [b_copy(mine, mine, 3, core)]
+            bias[0].start()
+        elif n == 1:
+            bias = dec_stage(dx_r, ordered(dcore, 2), x, 5, xpeer)
+        elif n == 2:
             bias = dec_stage(dz_r, ordered(dx_r, 4), z, 8, zpeer)
-        elif n == 1:
-            for copy in bias:
-                copy.wait()
+        else:
             bias = dec_stage(dy_r, ordered(dz_r, 4), y, 11, ypeer)
     stream_out.wait()
     enc.wait()
@@ -619,9 +616,10 @@
 def write_out(stream, own_grad, their_grad, enc, dec, stream_out, wgrad, enc_out, dec_out):
     zl = lax.axis_index("dp") % 2
     here = pl.ds(pl.multiple_of(zl * LAT, LAT), LAT)
-    there = pl.ds(pl.multiple_of((1 - zl) * LAT, LAT), LAT)
     wgrad[:, here] = own_grad[...]
-    wgrad[:, there] = their_grad[...].astype(F32)
+    for n in range(4):
+        there = pl.ds(pl.multiple_of((1 - zl) * LAT + n * 256, 256), 256)
+        wgrad[:, there] = their_grad[n].astype(F32)
 
     @pl.when(pl.program_id(0) == 0)
     def _():
@@ -641,7 +639,7 @@
         out_shape=(
             jax.ShapeDtypeStruct((ROWS, D), BF16),
             jax.ShapeDtypeStruct((OWN, LAT), F32),
-            jax.ShapeDtypeStruct((OWN, LAT), BF16),
+            jax.ShapeDtypeStruct((4, OWN, 256), BF16),
             jax.ShapeDtypeStruct((2, LAT), F32),
             jax.ShapeDtypeStruct((1, D), F32),
         ),
@@ -655,9 +653,9 @@
             pltpu.VMEM((3, 2, 4, 4, ROWS, QROWS), BF16),
             pltpu.VMEM((2, BATCH, LAT), F32),
             pltpu.VMEM((2, BATCH, LAT), BF16),
-            pltpu.VMEM((2, BATCH, LAT), BF16),
+            pltpu.VMEM((2, 4, BATCH, 256), BF16),
             pltpu.VMEM((3, 2, BATCH, LAT), BF16),
-            pltpu.VMEM((3, 2, BATCH, LAT), BF16),
+            pltpu.VMEM((3, 2, 4, BATCH, 256), BF16),
             pltpu.VMEM(block, BF16),
             pltpu.VMEM(block, F32),
             pltpu.VMEM(block, BF16),
@@ -668,7 +666,7 @@
             pltpu.VMEM((2, 4, ROWS, PART), BF16),
             pltpu.VMEM((2, 3, ROWS, PART), BF16),
             pltpu.VMEM((2, 3, ROWS, PART), BF16),
-            pltpu.VMEM((OWN, LAT), BF16),
+            pltpu.VMEM((4, OWN, 256), BF16),
             pltpu.VMEM((QROWS, 256), F32),
             pltpu.VMEM((2, ROWS, HALF), BF16),
             pltpu.VMEM((2, ROWS, HALF), BF16),
@@ -699,7 +697,7 @@
         attn_values.reshape(2, 4, 2, ROWS, 256),
         out_proj, post_gain, residual, sae_weight, enc_bias, dec_bias,
     )
-    steps = 6
+    steps = 3
 
     def fixed(*shape):
         return pl.BlockSpec(shape, lambda i: (0,) * len(shape))
@@ -717,7 +715,13 @@
                 jax.ShapeDtypeStruct((2 * LAT,), F32),
                 jax.ShapeDtypeStruct((D,), F32),
             ),
-            in_specs=[fixed(ROWS, D), rows(LAT), rows(LAT), fixed(2, LAT), fixed(1, D)],
+            in_specs=[
+                fixed(ROWS, D),
+                rows(LAT),
+                pl.BlockSpec((4, OWN // steps, 256), lambda i: (0, i, 0)),
+                fixed(2, LAT),
+                fixed(1, D),
+            ],
             out_specs=(fixed(ROWS, D), rows(2 * LAT), fixed(2 * LAT), fixed(D)),
         )(*parts)
     )

time: 174 us -> 169 us (0.971)
  Pallas kernels: 173 us -> 168 us
    pallas_call x1, Pallas kernels: 167 us -> 163 us  [per_device(): pl.pallas_call(kernel, out_shape=(jax.ShapeDtypeStruct((ROWS, D), BF16),...]
where the time goes in v4:
time: 169 us
  Pallas kernels  168 us (99%)
    pallas_call x1, Pallas kernels, per_device(): pl.pallas_call(kernel, out_shape=(jax.ShapeDtypeStruct((ROWS, D), BF16),...  163 us
    pallas_call x1, Pallas kernels, per_device(): pl.pallas_call(write_out, grid=(steps,), out_shape=(jax.ShapeDtypeStruct(...  4.98 us

profile of v4, /device:TPU:0, one launch (start us, length us, event | category | flops | bytes accessed | tf_op | source)
XLA Modules:
  0.0 168.6 jit_solution(13327643114148146096)
XLA Ops:
  0.6 163.0 %shard_map.102 = (bf16[16,4608]{1,0:T(8,128)(2,1)}, f32[576,1024]{1,0:T(8,128)}, bf16[4,576,256]{2,1,0:T(8,128)(2,1)}, f32[2,1024]{1,0:T(2,128)}, f32[1,4608]{1,0:T(1,128)}) custom-call(bf16[2,4,2,16,256]{4,3,2,1,0:T(8,128)(2,1)} %bitcast.1, bf16[256,4608]{1,0:T(8,128)(2,1)} %oproj.1, f32[4608]{0:T(1024)} %gain.1, bf16[16,4608]{1,0:T(8,128)(2,1)} %resid.1, ...), custom_call_target="tpu_custom_call" | custom-call | flops 24999999488 | bytes 20000000 | tf_op jit(solution)/shard_map/pallas_call | solution.py:637
  163.6 5.0 %shard_map.103 = (bf16[16,4608]{1,0:T(8,128)(2,1)}, f32[576,2048]{1,0:T(8,128)}, f32[2048]{0:T(1024)}, f32[4608]{0:T(1024)}) custom-call(bf16[16,4608]{1,0:T(8,128)(2,1)} %get-tuple-element.9.stream, f32[576,1024]{1,0:T(8,128)} %get-tuple-element.10.own_grad, bf16[4,576,256]{2,1,0:T(8,128)(2,1)} %get-tuple-element.11.their_grad, ...), custom_call_target="tpu_custom_call" | custom-call | tf_op jit(solution)/shard_map/pallas_call | solution.py:709

commit v5 on v4

--- a/solution.py
+++ b/solution.py
@@ -435,24 +435,24 @@
     cen_rows[1][3]()
     encode(1)
     lat_round[1][0]()
+    cen_part[1][2]()
     decode_peer(1)
     decode_own(1)
     recon_first(1)
-    cen_part[1][2]()
     lat_round[0][1]()
     dcore[pl.ds(c, 1), :] = jnp.zeros((1, D), F32)
     recon_second(0)
+    recon_second(1)
     cen_part[0][3]()
-    recon_second(1)
     error(0)
     err_rows[0][0]()
     err_part[0][0]()
     error(1)
     err_rows[1][0]()
     err_part[1][0]()
-    cen_part[1][3]()
     err_rows[0][1]()
     err_rows[1][1]()
+    cen_part[1][3]()
     lat_round[1][1]()
     err_part[0][1]()
     err_part[1][1]()

time: 169 us -> 164 us (0.970)
  Pallas kernels: 168 us -> 163 us
    pallas_call x1, Pallas kernels: 163 us -> 158 us  [per_device(): pl.pallas_call(kernel, out_shape=(jax.ShapeDtypeStruct((ROWS, D), BF16),...]
where the time goes in v5:
time: 164 us
  Pallas kernels  163 us (99%)
    pallas_call x1, Pallas kernels, per_device(): pl.pallas_call(kernel, out_shape=(jax.ShapeDtypeStruct((ROWS, D), BF16),...  158 us
    pallas_call x1, Pallas kernels, per_device(): pl.pallas_call(write_out, grid=(steps,), out_shape=(jax.ShapeDtypeStruct(...  4.98 us

profile of v5, /device:TPU:0, one launch (start us, length us, event | category | flops | bytes accessed | tf_op | source)
XLA Modules:
  0.0 163.9 jit_solution(15896048062417406080)
XLA Ops:
  0.6 158.3 %shard_map.102 = (bf16[16,4608]{1,0:T(8,128)(2,1)}, f32[576,1024]{1,0:T(8,128)}, bf16[4,576,256]{2,1,0:T(8,128)(2,1)}, f32[2,1024]{1,0:T(2,128)}, f32[1,4608]{1,0:T(1,128)}) custom-call(bf16[2,4,2,16,256]{4,3,2,1,0:T(8,128)(2,1)} %bitcast.1, bf16[256,4608]{1,0:T(8,128)(2,1)} %oproj.1, f32[4608]{0:T(1024)} %gain.1, bf16[16,4608]{1,0:T(8,128)(2,1)} %resid.1, ...), custom_call_target="tpu_custom_call" | custom-call | flops 24999999488 | bytes 20000000 | tf_op jit(solution)/shard_map/pallas_call | solution.py:637
  159.0 5.0 %shard_map.103 = (bf16[16,4608]{1,0:T(8,128)(2,1)}, f32[576,2048]{1,0:T(8,128)}, f32[2048]{0:T(1024)}, f32[4608]{0:T(1024)}) custom-call(bf16[16,4608]{1,0:T(8,128)(2,1)} %get-tuple-element.9.stream, f32[576,1024]{1,0:T(8,128)} %get-tuple-element.10.own_grad, bf16[4,576,256]{2,1,0:T(8,128)(2,1)} %get-tuple-element.11.their_grad, ...), custom_call_target="tpu_custom_call" | custom-call | tf_op jit(solution)/shard_map/pallas_call | solution.py:709
